TPU v7x, 32 devices: a whole 2x2x4 slice. The times are simulated.
32 devices in a mesh: batch: 4 (over z), tile: 8 (over y, x, core).
Axes of the slice: x: 2, y: 2, z: 4, core: 2. Of those that a mesh axis runs over, the one named last changes fastest.
Arguments:
- pixels: bfloat16 [4, 8, 8, 9, 36, 128], P('batch', 'tile'), may hold values from -6 to 6
- buckets: int32 [64], P('batch'), may hold values from 0 to 2
- slot_owner_table: int32 [328], replicated, may hold values from 0 to 327, each once
- out_grad: bfloat16 [4, 8, 2, 1, 18, 18, 320], P('batch', 'tile'), may hold values from -6 to 6
- master: float32 [328, 64, 64], P('tile'), may hold values from -0.25 to 0.25
- left_stat: float32 [328, 64, 64], P('tile'), as said below
- right_stat: float32 [328, 64, 64], P('tile'), as said below
- left_root: float32 [328, 64, 64], P('tile'), as said below
- right_root: float32 [328, 64, 64], P('tile'), as said below
- vectors: float32 [5248], replicated, may hold values from 0.5 to 1.5
- moment: float32 [5248], P('tile'), as said below
Outputs:
- result: float32 [4, 8, 2, 1, 18, 18, 320], P('batch', 'tile')
- pixel_grad: float32 [4, 8, 8, 9, 36, 128], P('batch', 'tile')
- clip_norm: float32 [], replicated
- block_grad: float32 [328, 64, 64], P('tile')
- left_new: float32 [328, 64, 64], P('tile')
- right_new: float32 [328, 64, 64], P('tile')
- master_new: float32 [328, 64, 64], P('tile')
- weight_copy: bfloat16 [328, 64, 64], P('tile')
- vec_grad: float32 [5248], P('tile')
- vec_moment: float32 [5248], P('tile')
- vec_new: float32 [5248], P('tile')
Inputs may be any that keep to these rules, and one draw needn't show every extreme that they name: `slot_owner_table`: slot s of the tile device p is entry p * 41 + s. `left_stat`: symmetric blocks with a positive diagonal. `right_stat`: symmetric blocks with a positive diagonal. `left_root`: symmetric blocks with a positive diagonal. `right_root`: symmetric blocks with a positive diagonal. `moment`: positive.
All inputs are finite; a program needn't handle non-finite values.
Results may differ from a plain program's by a relative error of at most 0.011.
Values may be sent and summed in bfloat16 or wider, within the bound.
No kernel may reach another device: no remote copies, remote signals or barrier semaphores. Data moves between devices by JAX's collectives and lax.ppermute only.
A program may use at most 576 MiB of HBM per device.

v0:
```python
import functools

import jax
import jax.numpy as jnp
from jax import lax
from jax.experimental import pallas as pl
from jax.experimental.layout import Layout, with_layout_constraint
from jax.experimental.pallas import tpu as pltpu
from jax.sharding import PartitionSpec as P

C2 = 128
HID2 = 512
C3 = 320
HID3 = 1280
CH = 36
CW = 36
STRIPS = 4
BS = 64
SR = CH // STRIPS
H3 = CH // 2
W3 = CW // 2
LONG = 7 * CH // 9
LINES = LONG // 2
WIDE = 384
LINE = 40
AREA = LINES * LINE
STEP = 2 * LINE
STEPS = AREA // STEP
HALF = BS // 2
STRIP = SR * CW
STRIP_ROWS = STRIP + -STRIP % 16

eps_norm = 1e-05
clip_limit = 1.0
rate_matrix = 0.3
rate_vector = 0.3
eps_adagrad = 1e-08
f32 = jnp.float32
bf16 = jnp.bfloat16

SHAPES = [(C2, HID2), (HID2, C2), (9 * C2, C3), (C3, HID3), (HID3, C3)]
USED = sum(rows // BS * (cols // BS) for rows, cols in SHAPES)
VEC_ROWS = (6 * C2 + HID2 + C2 + C3 + 6 * C3 + HID3 + C3) // 128


VEC_BLOCKS = -(-VEC_ROWS // HALF)


def extra_of(owned, groups):
    return VEC_BLOCKS + -(owned + VEC_BLOCKS) % groups


def product(left, right):
    return jnp.dot(left, right, preferred_element_type=f32)


def product_nt(left, right):
    return lax.dot_general(left, right, (((1,), (1,)), ((), ())), preferred_element_type=f32)


def product_tn(left, right):
    return lax.dot_general(left, right, (((0,), (0,)), ((), ())), preferred_element_type=f32)


def gelu_pair(values):
    bell = jnp.exp2(values * values * (-0.5 * 1.4426950408889634))
    step = pl.reciprocal(1.0 + (0.3275911 * 0.7071067811865476) * jnp.abs(values), approx=True)
    tail = step * (
        0.5 * 0.254829592
        + step
        * (
            0.5 * -0.284496736
            + step
            * (0.5 * 1.421413741 + step * (0.5 * -1.453152027 + step * (0.5 * 1.061405429)))
        )
    )
    tail = tail * bell
    share = jnp.where(values >= 0.0, 1.0 - tail, tail)
    return (values * share, share + values * (bell * 0.3989422804014327))


def fold(values):
    chans = values.shape[-1]
    return jnp.sum(values.reshape(-1, 8, chans), axis=0)


def by_image(total):
    total = total + pltpu.roll(total, 4, 0)
    total = total + pltpu.roll(total, 2, 0)
    return jnp.sum(total, axis=1, keepdims=True)


def line(pattern):
    return jnp.concatenate([pattern] * (LINE // 8), axis=0)


def spread(pattern, chans):
    return jnp.broadcast_to(pattern, (8, chans))


def affine(values, factor, shift):
    tiles = values.reshape(-1, 8, values.shape[-1])
    return (tiles * factor + shift).reshape(values.shape)


def scaled(values, factor):
    tiles = values.reshape(-1, 8, values.shape[-1])
    return (tiles * factor).reshape(values.shape)


def from_left(values):
    return pltpu.roll(values, 2, 0)


def from_right(values):
    return pltpu.roll(values, values.shape[0] - 2, 0)


def rounded(values):
    return values.astype(bf16).astype(f32)


def widen(values):
    return jnp.concatenate([values] * (WIDE // 128), axis=-1)


def norm_terms(total, square, count):
    mean = by_image(total) / count
    scaling = lax.rsqrt(by_image(square) / count - mean * mean + eps_norm)
    return (mean, scaling)


def sweep(visit, start):
    return lax.fori_loop(0, STEPS, visit, start, unroll=True)


def step_rows(k, lines=0):
    start = k * STEP + lines * LINE
    return pl.ds(start if isinstance(k, int) else pl.multiple_of(start, LINE), STEP)


def held_in(space, *arrays):
    return [pltpu.with_memory_space_constraint(array, space) for array in arrays]


VMEM_BLOCK = pl.BlockSpec(memory_space=pltpu.VMEM)
HBM = pl.BlockSpec(memory_space=pltpu.HBM)
SMEM = pl.BlockSpec(memory_space=pltpu.SMEM)


def roomy(mebibytes):
    return pltpu.CompilerParams(vmem_limit_bytes=mebibytes * 1024 * 1024)


def image_shape(bucket_of, pair, image):
    bucket = bucket_of(2 * pair + image)
    plain = jnp.where(bucket == 0, 5 * CH // 9, 7 * CH // 9)
    across = jnp.where(bucket == 0, CW, 7 * CW // 9)
    turned = (bucket >= 2).astype(jnp.int32)
    return (
        jnp.where(turned > 0, 5 * CW // 9, plain),
        jnp.where(turned > 0, CH, across),
        turned,
    )


def bucket_reader(place_ref, bucket_ref, strip_count):
    return lambda group: bucket_ref[group * strip_count + place_ref[0]]


class Geometry:
    def __init__(self, bucket_of, pair):
        parity = lax.broadcasted_iota(jnp.int32, (8, 128), 0) % 2
        even, odd = (image_shape(bucket_of, pair, image) for image in range(2))
        high, broad, turned = (jnp.where(parity == 0, a, b) for a, b in zip(even, odd))
        self.high = high
        self.count_two = (high * broad * C2).astype(f32)[:, :1]
        self.high3 = (high + 1) // 2
        broad3 = (broad + 1) // 2
        self.count_three = (self.high3 * broad3 * C3).astype(f32)[:, :1]
        place = lax.broadcasted_iota(jnp.int32, (LINE, 128), 0) // 2
        inside = lax.broadcasted_iota(jnp.int32, (LINE, 128), 0) < 2 * W3
        self.reach = []
        self.col_share = []
        for pc in range(2):
            column = 2 * place + pc
            self.reach.append(jnp.where(inside & (column < line(broad)), line(high), 0))
            edge = (column == 0) | (column == line(broad) - 1)
            self.col_share.append(jnp.where(edge, 0.5, 1.0 / 3.0))
        self.reach3 = jnp.where(inside & (place < line(broad3)), line(self.high3), 0)
        edge3 = (place == 0) | (place == line(broad3) - 1)
        self.col_share3 = jnp.where(edge3, 0.5, 1.0 / 3.0)
        self.flipped = jnp.concatenate([turned] * (STEP // 8), axis=0) > 0

    def share(self, plane, k):
        pr, pc = plane // 2, plane % 2
        return self.lines(4 * k + pr, 2, self.reach[pc], self.col_share[pc], self.high)

    def share3(self, k):
        return self.lines(2 * k, 1, self.reach3, self.col_share3, self.high3)

    def lines(self, row, stride, reach, col_share, height):
        parts = []
        for n in range(2):
            here = row + stride * n
            row_share = jnp.where((here == 0) | (here == height - 1), 0.5, 1.0 / 3.0)
            parts.append(jnp.where(here < reach, line(row_share) * col_share, 0.0))
        return jnp.concatenate(parts, axis=0)


def strip_place(pair, spot, strip_count):
    return lax.rem(pair * 8 + strip_count - 2 + spot, strip_count)


def each_image(bucket_of, pair, visit):
    for image in range(2):
        way = image_shape(bucket_of, pair, image)[2]

        @pl.when(way == 0)
        def _():
            def one(r, carry):
                for plane in range(4):
                    row = 2 * r + plane // 2
                    strip = row // SR
                    there = pl.ds((row - strip * SR) * CW + plane % 2, W3, stride=2)
                    here = pl.ds(r * LINE + image, W3, stride=2)
                    visit(plane, here, image * STRIPS + strip, there)
                return carry

            lax.fori_loop(0, LINES, one, 0)

        @pl.when(way == 1)
        def _():
            def one(r, carry):
                for plane in range(4):
                    for strip in range(STRIPS):
                        first = (plane % 2 + strip * SR) % 2
                        count = (SR - first + 1) // 2
                        done = (strip * SR + first) // 2
                        column = 2 * r + plane // 2
                        there = pl.ds(first * CW + column, count, stride=2 * CW)
                        here = pl.ds(r * LINE + image + 2 * done, count, stride=2)
                        visit(plane, here, image * STRIPS + strip, there)
                return carry

            lax.fori_loop(0, LINES, one, 0)


def row_windows(col_ref, pc, k):
    both = col_ref[pc, step_rows(k, 1)] + col_ref[2 + pc, step_rows(k, 1)]
    return (both + col_ref[2 + pc, step_rows(k)], both + col_ref[pc, step_rows(k, 2)])


def put_col_windows(col_ref, pr, k, even, odd):
    both = even + odd
    col_ref[pr * 2, step_rows(k, 1)] = both + from_left(odd)
    col_ref[pr * 2 + 1, step_rows(k, 1)] = both + from_right(even)


def clear_edges(col_ref):
    zero_line = jnp.zeros((LINE, C2), f32)
    for plane in range(4):
        col_ref[plane, 0:LINE] = zero_line
        col_ref[plane, AREA + LINE : AREA + 2 * LINE] = zero_line


def entry_kernel(pairs, strip_count, piece_count, place_ref, bucket_ref, vec_ref, *refs):
    piece_refs, refs = refs[:piece_count], refs[piece_count:]
    x_out, inv_out, pool_out, mix_out, stat_out, image_ref, col_ref = refs
    pair = pl.program_id(0) if pairs > 1 else 0
    x_ref, inv_ref, pool_ref, mix_ref = (ref.at[0] for ref in (x_out, inv_out, pool_out, mix_out))
    bucket_of = bucket_reader(place_ref, bucket_ref, strip_count)
    shape = Geometry(bucket_of, pair)
    gain1, bias1, scale1 = (vec_ref[n : n + 1] for n in range(3))
    clear_edges(col_ref)
    if piece_count > 1:
        half = piece_count // 2
        for n, ref in enumerate(piece_refs):
            source = place_ref[0] ^ (n // half + 2 * (n % half))
            spot = lax.rem(source + 2, 2 * STRIPS)
            first = 0 if n < half else ref.shape[0] - STRIP_ROWS
            image_ref[spot] = ref[first : first + STRIP_ROWS].astype(f32)
    else:
        for spot in range(2 * STRIPS):
            source = strip_place(pair, spot, strip_count)
            image_ref[spot] = piece_refs[0][source].astype(f32)

    def take_in(plane, here, spot, there):
        x_ref[plane, here] = image_ref[spot, there]

    each_image(bucket_of, pair, take_in)

    def arrange(k, carry):
        total, square = carry
        rows = step_rows(k)
        for plane in range(4):
            share = shape.share(plane, k)
            inv_ref[plane, rows] = share
            values = jnp.where(share > 0.0, x_ref[plane, rows], 0.0)
            x_ref[plane, rows] = values
            total = total + fold(values)
            square = square + fold(values * values)
        return (total, square)

    nothing = jnp.zeros((8, C2), f32)
    total, square = sweep(arrange, (nothing, nothing))
    mean1, scaling1 = norm_terms(total, square, shape.count_two)
    factor1 = scaling1 * gain1
    shift1 = bias1 - mean1 * scaling1 * gain1

    def window_cols(k, carry):
        rows = step_rows(k)
        for pr in range(2):
            masked = []
            for pc in range(2):
                plane = pr * 2 + pc
                normal = rounded(affine(x_ref[plane, rows], factor1, shift1))
                masked.append(jnp.where(inv_ref[plane, rows] > 0.0, normal, 0.0))
            put_col_windows(col_ref, pr, k, *masked)
        return carry

    sweep(window_cols, 0)

    def mix(k, carry):
        total, square = carry
        rows = step_rows(k)
        for pc in range(2):
            windows = row_windows(col_ref, pc, k)
            for pr in range(2):
                plane = pr * 2 + pc
                values = x_ref[plane, rows]
                share = inv_ref[plane, rows]
                pooled = windows[pr] * share - rounded(affine(values, factor1, shift1))
                pooled = jnp.where(share > 0.0, pooled, 0.0)
                mixed = values + scale1 * pooled
                pool_ref[plane, rows] = pooled
                mix_ref[plane, rows] = mixed
                total = total + fold(mixed)
                square = square + fold(mixed * mixed)
        return (total, square)

    total, square = sweep(mix, (nothing, nothing))
    mean2, scaling2 = norm_terms(total, square, shape.count_two)
    for n, value in enumerate((mean1, scaling1, mean2, scaling2)):
        stat_out[0, n] = spread(value, 128)


def pair_specs(pairs, shapes, mode=None):
    if pairs == 1:
        return [VMEM_BLOCK] * len(shapes)
    return [
        pl.BlockSpec(
            (1,) + shape, lambda t, rank=len(shape): (t,) + (0,) * rank, pipeline_mode=mode
        )
        for shape in shapes
    ]


def whole_specs(pairs, shapes):
    if pairs == 1:
        return [VMEM_BLOCK] * len(shapes)
    return [
        pl.BlockSpec(
            shape,
            lambda t, rank=len(shape): (0,) * rank,
            pipeline_mode=pl.Buffered(1),
        )
        for shape in shapes
    ]


def pair_arrays(pairs, shapes, kinds):
    make = pltpu.VMEM if pairs == 1 else jax.ShapeDtypeStruct
    return [make((pairs,) + shape, kind) for shape, kind in zip(shapes, kinds)]


STATE = [(4, AREA, C2)] * 4 + [(4, 8, 128)]
BACK = [(4, AREA, C2)] * 2 + [(2, 8, 128)]


def run_entry(place, buckets, pieces, vec, strip_count):
    pairs = strip_count // 8
    if pairs == 1:
        pieces = held_in(pltpu.VMEM, *pieces)
    return pl.pallas_call(
        functools.partial(entry_kernel, pairs, strip_count, len(pieces)),
        grid=() if pairs == 1 else (pairs,),
        in_specs=[SMEM] * 2 + whole_specs(pairs, [array.shape for array in (vec, *pieces)]),
        out_specs=pair_specs(pairs, STATE),
        out_shape=pair_arrays(pairs, STATE, [f32] * 5),
        scratch_shapes=[
            pltpu.VMEM((2 * STRIPS, STRIP_ROWS, C2), f32),
            pltpu.VMEM((4, AREA + 2 * LINE, C2), f32),
        ],
        compiler_params=roomy(6 if pairs == 1 else 40),
        name="entry",
    )(place, buckets, vec, *pieces)


WEIGHTS = [(C2, HID2), (HID2, C2), (9 * C2, WIDE), (WIDE, HID3), (HID3, WIDE)]


def unpack_kernel(spans, slot_ref, *refs):
    piece_refs, refs = refs[: len(spans)], refs[len(spans) :]
    weights, gathered_ref = refs[:-1], refs[-1]
    done = 0
    for ref, (first, count) in zip(piece_refs, spans):
        blocks = ref[first : first + count * HALF].reshape(count, HALF, 128)
        gathered_ref[done : done + count] = blocks
        done += count
    left_half = lax.broadcasted_iota(jnp.int32, (HALF, 128), 1) < BS
    offset = 0
    for (rows, cols), ref in zip(SHAPES, weights):
        wide = cols // BS
        for rb in range(rows // BS):
            for cb in range(0, wide, 2):
                number = offset + rb * wide + cb
                first = gathered_ref[slot_ref[number]]
                turned = pltpu.roll(first, BS, 1)
                if cb + 1 < wide:
                    second = gathered_ref[slot_ref[number + 1]]
                    top = jnp.where(left_half, first, pltpu.roll(second, BS, 1))
                    low = jnp.where(left_half, turned, second)
                else:
                    top = jnp.where(left_half, first, 0.0)
                    low = jnp.where(left_half, turned, 0.0)
                place = slice(cb * BS, cb * BS + 128)
                ref[rb * BS : rb * BS + HALF, place] = top
                ref[rb * BS + HALF : rb * BS + BS, place] = low
        offset += rows // BS * wide
    weights[3][C3:, :] = jnp.zeros((WIDE - C3, HID3), bf16)


def run_unpack(slot_of, pieces, spans):
    slots = slot_of.shape[0]
    return pl.pallas_call(
        functools.partial(unpack_kernel, spans),
        in_specs=[SMEM] + [VMEM_BLOCK] * len(pieces),
        out_specs=[VMEM_BLOCK] * 5,
        out_shape=[pltpu.VMEM(shape, bf16) for shape in WEIGHTS],
        scratch_shapes=[pltpu.VMEM((slots, HALF, 128), bf16)],
        compiler_params=roomy(6),
        name="unpack",
    )(slot_of, *held_in(pltpu.VMEM, *pieces))


def main_kernel(
    pairs,
    strip_count,
    slots,
    near_place,
    far_place,
    place_ref,
    bucket_ref,
    inv_in,
    mix_in,
    stat_in,
    goal_ref,
    vec_ref,
    w1_ref,
    w2_ref,
    we_ref,
    w3_ref,
    w4_ref,
    result_ref,
    zed_out,
    dx_out,
    mean_out,
    near_ref,
    far_ref,
    flat_ref,
    zed_ref,
    hid_ref,
    u_ref,
    g_ref,
    h_ref,
    dy_ref,
    patch_ref,
    dpatch_ref,
    inv3_ref,
    e_ref,
    col3_ref,
    pool3_ref,
    mix3_ref,
    dx3_ref,
    hid3_ref,
    dhid3_ref,
    u3_ref,
    g3_ref,
    h3_ref,
    dy3_ref,
    dpre_ref,
    gw1_ref,
    gw2_ref,
    gwe_ref,
    gw3_ref,
    gw4_ref,
    acc_two,
    acc_hid_two,
    acc_three,
    acc_hid_three,
):
    pair = pl.program_id(0) if pairs > 1 else 0
    grads = [gw1_ref, gw2_ref, gwe_ref, gw3_ref, gw4_ref]
    inv_ref, mix_ref, stat_ref = (ref.at[0] for ref in (inv_in, mix_in, stat_in))
    back_ref, dx_ref = zed_out.at[0], dx_out.at[0]
    left_half = lax.broadcasted_iota(jnp.int32, (HALF, 128), 1) < BS

    def at_pair(number, act):
        if pairs == 1:
            act()
        else:
            pl.when(pair == number)(act)

    def begin():
        acc_two[...] = jnp.zeros(acc_two.shape, f32)
        acc_hid_two[...] = jnp.zeros(acc_hid_two.shape, f32)
        acc_three[...] = jnp.zeros(acc_three.shape, f32)
        acc_hid_three[...] = jnp.zeros(acc_hid_three.shape, f32)

    at_pair(0, begin)
    shape = Geometry(bucket_reader(place_ref, bucket_ref, strip_count), pair)
    count_two, count_three, flipped = shape.count_two, shape.count_three, shape.flipped
    nothing = jnp.zeros((8, C2), f32)
    nothing3 = jnp.zeros((8, WIDE), f32)

    def vector_row(at, length):
        first, shift = at // 128, at % 128
        count = -(-(shift + length) // 128)
        row = jnp.concatenate([vec_ref[first + n : first + n + 1] for n in range(count)], axis=1)
        if shift:
            row = pltpu.roll(jnp.broadcast_to(row, (8, count * 128)), count * 128 - shift, 1)[:1]
        return row

    def wide_row(at):
        lane = lax.broadcasted_iota(jnp.int32, (1, WIDE), 1)
        return jnp.where(lane < C3, vector_row(at, C3)[:, :WIDE], 0.0)

    gain2, bias2, scale2 = (vec_ref[n : n + 1] for n in range(3, 6))
    hid_bias = vector_row(6 * C2, HID2)
    out_bias = vector_row(6 * C2 + HID2, C2)
    two = 7 * C2 + HID2
    embed_bias, gain3, bias3, scale3 = (wide_row(two + n * C3) for n in range(4))
    gain4, bias4, scale4 = (wide_row(two + n * C3) for n in range(4, 7))
    hid_bias3 = vector_row(two + 7 * C3, HID3)[:, :HID3]
    out_bias3 = wide_row(two + 7 * C3 + HID3)
    mean2, scaling2 = stat_ref[2], stat_ref[3]
    factor2 = scaling2 * gain2
    shift2 = bias2 - mean2 * scaling2 * gain2
    for plane in range(4):
        zed_ref[plane, 0:LINE] = jnp.zeros((LINE, C2), f32)
    col3_ref[0:LINE] = jnp.zeros((LINE, WIDE), f32)
    col3_ref[AREA + LINE : AREA + 2 * LINE] = jnp.zeros((LINE, WIDE), f32)

    def put_block(number, block):
        near_ref[near_place[number]] = block
        far_ref[far_place[number]] = block

    offsets = [0]
    for rows, cols in SHAPES:
        offsets.append(offsets[-1] + rows // BS * (cols // BS))

    def pack_part(which, values, row=0, col=0):
        rows, cols = SHAPES[which]
        wide = cols // BS
        values = values.astype(bf16)
        for rb in range(row // BS, min(rows, row + values.shape[0]) // BS):
            for cb in range(col // BS, min(cols, col + values.shape[1]) // BS, 2):
                number = offsets[which] + rb * wide + cb
                start = rb * BS - row
                at = slice(cb * BS - col, cb * BS - col + 128)
                top = values[start : start + HALF, at]
                low = values[start + HALF : start + BS, at]
                put_block(number, jnp.where(left_half, top, pltpu.roll(low, BS, 1)))
                if cb + 1 < wide:
                    put_block(number + 1, jnp.where(left_half, pltpu.roll(top, BS, 1), low))

    def plane_rows(plane):
        return slice(plane * AREA, plane * AREA + AREA)

    def begin_plane(plane):
        low = affine(mix_ref[plane], factor2, shift2).astype(bf16)
        h_ref[plane_rows(plane)] = low
        hid_ref[plane % 2] = product(low, w1_ref[...])

    begin_plane(0)
    for plane in range(4):
        if plane < 3:
            begin_plane(plane + 1)
        for k in range(STEPS):
            rows = step_rows(k)
            flat = slice(plane * AREA + k * STEP, plane * AREA + k * STEP + STEP)
            for at in range(0, HID2, 128):
                lanes = slice(at, at + 128)
                active, slope = gelu_pair(hid_ref[plane % 2, rows, lanes] + hid_bias[:, lanes])
                u_ref[flat, lanes] = active.astype(bf16)
                g_ref[flat, lanes] = slope.astype(bf16)
        out = product(u_ref[plane_rows(plane)], w2_ref[...]) + out_bias
        zed = jnp.where(inv_ref[plane] > 0.0, mix_ref[plane] + scale2 * out, 0.0)
        zed_ref[plane, LINE : LINE + AREA] = rounded(zed)

    def patches(k, carry):
        rows = step_rows(k)
        taps = []
        for ky in range(3):
            pr = (0 if ky == 1 else 1) * 2
            source = step_rows(k, 0 if ky == 0 else 1)
            even = zed_ref[pr, source]
            odd = zed_ref[pr + 1, source]
            taps.append((from_left(odd), even, odd))
        for ky in range(3):
            for kx in range(3):
                at = (3 * ky + kx) * C2
                tap = taps[ky][kx]
                if ky != kx:
                    tap = jnp.where(flipped, taps[kx][ky], tap)
                patch_ref[rows, at : at + C2] = tap.astype(bf16)
        return carry

    sweep(patches, 0)
    e_ref[...] = product(patch_ref[...], we_ref[...])

    def embed(k, carry):
        total, square = carry
        rows = step_rows(k)
        share = shape.share3(k)
        inv3_ref[rows] = share
        out = jnp.where(widen(share) > 0.0, e_ref[rows] + embed_bias, 0.0)
        e_ref[rows] = out
        return (total + fold(out), square + fold(out * out))

    total, square = sweep(embed, (nothing3, nothing3))
    mean3, scaling3 = norm_terms(total, square, count_three)
    factor3 = scaling3 * gain3
    shift3 = bias3 - mean3 * scaling3 * gain3

    def window_cols3(k, carry):
        rows = step_rows(k)
        normal = rounded(affine(e_ref[rows], factor3, shift3))
        masked = jnp.where(widen(inv3_ref[rows]) > 0.0, normal, 0.0)
        col3_ref[step_rows(k, 1)] = masked + from_left(masked) + from_right(masked)
        return carry

    sweep(window_cols3, 0)

    def row_windows3(k):
        return col3_ref[step_rows(k)] + col3_ref[step_rows(k, 1)] + col3_ref[step_rows(k, 2)]

    def mix3(k, carry):
        total, square = carry
        rows = step_rows(k)
        values = e_ref[rows]
        share = widen(inv3_ref[rows])
        pooled = row_windows3(k) * share - rounded(affine(values, factor3, shift3))
        pooled = jnp.where(share > 0.0, pooled, 0.0)
        mixed = values + scale3 * pooled
        pool3_ref[rows] = pooled
        mix3_ref[rows] = mixed
        return (total + fold(mixed), square + fold(mixed * mixed))

    total, square = sweep(mix3, (nothing3, nothing3))
    mean4, scaling4 = norm_terms(total, square, count_three)
    factor4 = scaling4 * gain4
    shift4 = bias4 - mean4 * scaling4 * gain4
    normal4 = (spread(scaling4, WIDE), spread(-mean4 * scaling4, WIDE))

    def prepare3(k, d_bias):
        rows = step_rows(k)
        h3_ref[rows] = affine(mix3_ref[rows], factor4, shift4).astype(bf16)
        goal = goal_ref[0, rows].astype(f32)
        goal = jnp.where(widen(inv3_ref[rows]) > 0.0, goal, 0.0)
        goal = scale4 * goal
        dy3_ref[rows] = goal.astype(bf16)
        return d_bias + fold(goal)

    acc_three[7] += sweep(prepare3, nothing3)

    def keep(which, value, row=0, col=0):
        if pairs == 1:
            pack_part(which, value, row, col)
        else:
            ref = grads[which]
            place = (slice(row, row + value.shape[0]), slice(col, col + value.shape[1]))

            @pl.when(pair == 0)
            def _():
                ref[place] = value

            @pl.when(pair > 0)
            def _():
                ref[place] += value

    def begin_chunk(at):
        lanes = slice(at, at + 256)
        hid3_ref[:, lanes] = product(h3_ref[...], w3_ref[:, lanes])
        dhid3_ref[:, lanes] = product_nt(dy3_ref[...], w4_ref[lanes])

    begin_chunk(0)
    for at in range(0, HID3, 256):
        if at + 256 < HID3:
            begin_chunk(at + 256)
        for lane in (at, at + 128):
            lanes = slice(lane, lane + 128)
            total = nothing
            for k in range(STEPS):
                rows = step_rows(k)
                active, slope = gelu_pair(hid3_ref[rows, lanes] + hid_bias3[:, lanes])
                u3_ref[rows, lanes] = active.astype(bf16)
                change = slope * dhid3_ref[rows, lanes]
                g3_ref[rows, lanes] = change.astype(bf16)
                total = total + fold(change)
            acc_hid_three[:, lanes] += total
        lanes = slice(at, at + 256)
        out = product(u3_ref[:, lanes], w4_ref[lanes])
        d_low = product_nt(g3_ref[:, lanes], w3_ref[:, lanes])
        result_ref[0] = out if at == 0 else result_ref[0] + out
        dx3_ref[...] = d_low if at == 0 else dx3_ref[...] + d_low
        keep(3, product_tn(h3_ref[...], g3_ref[:, lanes]), col=at)
        keep(4, product_tn(u3_ref[:, lanes], dy3_ref[...]), row=at)

    def finish3(k, carry):
        d_scale, d_shift, d_gain = carry
        rows = step_rows(k)
        valid = widen(inv3_ref[rows]) > 0.0
        mixed = mix3_ref[rows]
        out = jnp.where(valid, result_ref[0, rows] + out_bias3, 0.0)
        result_ref[0, rows] = mixed + scale4 * out
        d_scale = d_scale + fold(out * goal_ref[0, rows].astype(f32))
        d_low = dx3_ref[rows]
        normal = affine(mixed, *normal4)
        return (d_scale, d_shift + fold(d_low), d_gain + fold(d_low * normal))

    d_scale, d_shift, d_gain = sweep(finish3, (nothing3, nothing3, nothing3))
    acc_three[6] += d_scale
    acc_three[5] += d_shift
    acc_three[4] += d_gain
    mean_shift = by_image(d_shift * gain4) / count_three
    mean_gain = by_image(d_gain * gain4) / count_three
    back_gain4 = scaling4 * gain4
    back_mean4 = spread(-scaling4 * mean_shift, WIDE)
    back_normal4 = spread(scaling4 * mean_gain, WIDE)

    def unmix3(k, d_scale):
        rows = step_rows(k)
        share = widen(inv3_ref[rows])
        valid = share > 0.0
        normal = affine(mix3_ref[rows], *normal4)
        back = affine(dx3_ref[rows], back_gain4, back_mean4) - scaled(normal, back_normal4)
        d_mixed = jnp.where(valid, back + goal_ref[0, rows].astype(f32), 0.0)
        dx3_ref[rows] = d_mixed
        d_scale = d_scale + fold(pool3_ref[rows] * d_mixed)
        weighted = scale3 * d_mixed * share
        col3_ref[step_rows(k, 1)] = weighted + from_left(weighted) + from_right(weighted)
        return d_scale

    acc_three[3] += sweep(unmix3, nothing3)
    normal3 = (spread(scaling3, WIDE), spread(-mean3 * scaling3, WIDE))

    def unpool3(k, carry):
        d_shift, d_gain = carry
        rows = step_rows(k)
        valid = widen(inv3_ref[rows]) > 0.0
        d_normal = jnp.where(valid, row_windows3(k) - scale3 * dx3_ref[rows], 0.0)
        pool3_ref[rows] = d_normal
        normal = affine(e_ref[rows], *normal3)
        return (d_shift + fold(d_normal), d_gain + fold(d_normal * normal))

    d_shift, d_gain = sweep(unpool3, (nothing3, nothing3))
    acc_three[2] += d_shift
    acc_three[1] += d_gain
    mean_shift = by_image(d_shift * gain3) / count_three
    mean_gain = by_image(d_gain * gain3) / count_three
    back_gain3 = scaling3 * gain3
    back_mean3 = spread(-scaling3 * mean_shift, WIDE)
    back_normal3 = spread(scaling3 * mean_gain, WIDE)

    def unnorm3(k, d_bias):
        rows = step_rows(k)
        valid = widen(inv3_ref[rows]) > 0.0
        normal = affine(e_ref[rows], *normal3)
        back = affine(pool3_ref[rows], back_gain3, back_mean3) - scaled(normal, back_normal3)
        low = jnp.where(valid, dx3_ref[rows] + back, 0.0).astype(bf16)
        dpre_ref[rows] = low
        return d_bias + fold(low.astype(f32))

    acc_three[0] += sweep(unnorm3, nothing3)
    keep(2, product_tn(patch_ref[...], dpre_ref[...]))
    dpatch_ref[0:AREA] = product_nt(dpre_ref[...], we_ref[...])
    dpatch_ref[AREA : AREA + LINE] = jnp.zeros((LINE, 9 * C2), f32)

    def gather_back(k, carry):
        rows = step_rows(k)

        def tap(ky, kx, source):
            at = (3 * ky + kx) * C2
            value = dpatch_ref[source, at : at + C2]
            if ky != kx:
                at = (3 * kx + ky) * C2
                value = jnp.where(flipped, dpatch_ref[source, at : at + C2], value)
            return value

        sources = []
        for ky in range(3):
            source = step_rows(k, 1 if ky == 0 else 0)
            sources.append(
                (tap(ky, 1, source), tap(ky, 2, source) + from_right(tap(ky, 0, source)))
            )
        for pc in range(2):
            for pr, value in ((0, sources[1][pc]), (1, sources[2][pc] + sources[0][pc])):
                plane = pr * 2 + pc
                valid = inv_ref[plane, rows] > 0.0
                back_ref[plane, rows] = jnp.where(valid, rounded(value), 0.0)
        return carry

    sweep(gather_back, 0)

    normal2 = (spread(scaling2, C2), spread(-mean2 * scaling2, C2))

    def begin_back(plane):
        goal = scale2 * back_ref[plane]
        dy_ref[plane_rows(plane)] = goal.astype(bf16)
        hid_ref[plane % 2] = product_nt(goal.astype(bf16), w2_ref[...])
        return fold(goal)

    d_out_bias = begin_back(0)
    d_shift, d_gain = nothing, nothing
    sums = [nothing] * (HID2 // 128)
    new_gw1, new_gw2 = None, None
    for plane in range(4):
        if plane < 3:
            d_out_bias = d_out_bias + begin_back(plane + 1)
        for k in range(STEPS):
            rows = step_rows(k)
            part = slice(plane * AREA + k * STEP, plane * AREA + k * STEP + STEP)
            for n, at in enumerate(range(0, HID2, 128)):
                lanes = slice(at, at + 128)
                change = g_ref[part, lanes].astype(f32) * hid_ref[plane % 2, rows, lanes]
                g_ref[part, lanes] = change.astype(bf16)
                sums[n] = sums[n] + fold(change)
        flat = plane_rows(plane)
        d_low = product_nt(g_ref[flat], w1_ref[...])
        dx_ref[plane] = d_low
        d_shift = d_shift + fold(d_low)
        d_gain = d_gain + fold(d_low * affine(mix_ref[plane], *normal2))
        part_gw1 = product_tn(h_ref[flat], g_ref[flat])
        part_gw2 = product_tn(dy_ref[flat], u_ref[flat])
        new_gw1 = part_gw1 if plane == 0 else new_gw1 + part_gw1
        new_gw2 = part_gw2 if plane == 0 else new_gw2 + part_gw2
    new_gw2 = new_gw2.T
    for n, value in enumerate(sums):
        acc_hid_two[:, n * 128 : n * 128 + 128] += value
    acc_two[6] += d_out_bias
    acc_two[4] += d_shift
    acc_two[3] += d_gain
    mean_out[0, 0] = spread(by_image(d_shift * gain2) / count_two, 128)
    mean_out[0, 1] = spread(by_image(d_gain * gain2) / count_two, 128)
    keep(0, new_gw1)
    keep(1, new_gw2)
    d_scale = fold(w2_ref[...].astype(f32) * new_gw2) + out_bias * d_out_bias
    acc_two[5] += d_scale / scale2

    def finish():
        if pairs > 1:
            for which, ref in enumerate(grads):
                pack_part(which, ref[...])

        def filler(number, carry):
            put_block(number, jnp.zeros((HALF, 128), bf16))
            return carry

        lax.fori_loop(USED, slots, filler, 0)

        flat_ref[...] = jnp.zeros(flat_ref.shape, f32)

        def put(at, total, length):
            if at % 128:
                room = jnp.zeros((8, 128), f32)
                if total.shape[1] < length + BS:
                    total = jnp.concatenate([total, room], axis=1)
                total = pltpu.roll(total, BS, 1)
            whole = jnp.sum(total, axis=0, keepdims=True)
            done = -(at % 128)
            row = at // 128
            lane = 0
            while done < length:
                first = max(0, -done)
                last = min(128, length - done)
                flat_ref[row : row + 1, first:last] = whole[:, lane + first : lane + last]
                done += 128
                lane += 128
                row += 1

        at = 3 * C2
        for n in range(3, 6):
            put(at, acc_two[n], C2)
            at += C2
        put(at, acc_hid_two[...], HID2)
        at += HID2
        put(at, acc_two[6], C2)
        at += C2
        for n in range(7):
            put(at, acc_three[n], C3)
            at += C3
        put(at, acc_hid_three[...], HID3)
        at += HID3
        put(at, acc_three[7], C3)

    at_pair(pairs - 1, finish)


def run_main(places, place, buckets, state, goal, vec, weights, strip_count):
    pairs = goal.shape[0]
    slots = places[0].shape[0]
    half = slots // 2 + 1
    if pairs == 1:
        state = held_in(pltpu.VMEM, *state)
    weights = held_in(pltpu.VMEM, *weights)
    _, inv, _, mix, stat = state
    state_shapes = [STATE[1], STATE[3], STATE[4]]
    wide_f32 = pltpu.VMEM((AREA, WIDE), f32)
    wide_bf16 = pltpu.VMEM((AREA, WIDE), bf16)
    scratch = [
        pltpu.VMEM((4, AREA + LINE, C2), f32),
        pltpu.VMEM((2, AREA, HID2), f32),
        pltpu.VMEM((4 * AREA, HID2), bf16),
        pltpu.VMEM((4 * AREA, HID2), bf16),
        pltpu.VMEM((4 * AREA, C2), bf16),
        pltpu.VMEM((4 * AREA, C2), bf16),
        pltpu.VMEM((AREA, 9 * C2), bf16),
        pltpu.VMEM((AREA + LINE, 9 * C2), f32),
        pltpu.VMEM((AREA, 128), f32),
        wide_f32,
        pltpu.VMEM((AREA + 2 * LINE, WIDE), f32),
        wide_f32,
        wide_f32,
        wide_f32,
        pltpu.VMEM((AREA, HID3), f32),
        pltpu.VMEM((AREA, HID3), f32),
        pltpu.VMEM((AREA, HID3), bf16),
        pltpu.VMEM((AREA, HID3), bf16),
        wide_bf16,
        wide_bf16,
        wide_bf16,
        *[pltpu.VMEM(shape if pairs > 1 else (8, 128), f32) for shape in WEIGHTS],
        pltpu.VMEM((7, 8, C2), f32),
        pltpu.VMEM((8, HID2), f32),
        pltpu.VMEM((8, 8, WIDE), f32),
        pltpu.VMEM((8, HID3), f32),
    ]
    out_shapes = [(half, HALF, 128), (half, HALF, 128), (VEC_BLOCKS * HALF, 128)]
    make = pltpu.VMEM if pairs == 1 else jax.ShapeDtypeStruct
    return pl.pallas_call(
        functools.partial(main_kernel, pairs, strip_count, slots),
        grid=() if pairs == 1 else (pairs,),
        in_specs=[SMEM] * 4
        + pair_specs(pairs, state_shapes + [goal.shape[1:]], pl.Buffered(1))
        + whole_specs(pairs, [vec.shape])
        + [VMEM_BLOCK] * 5,
        out_specs=pair_specs(pairs, [(AREA, WIDE)] + BACK) + whole_specs(pairs, out_shapes),
        out_shape=pair_arrays(pairs, [(AREA, WIDE)] + BACK, [f32] * 4)
        + [make(shape, kind) for shape, kind in zip(out_shapes, (bf16, bf16, f32))],
        scratch_shapes=scratch,
        compiler_params=pltpu.CompilerParams(
            vmem_limit_bytes=(40 if pairs == 1 else 56) * 1024 * 1024,
        ),
        name="blocks",
    )(*places, place, buckets, inv, mix, stat, goal, vec, *weights)


def exit_kernel(
    pairs,
    strip_count,
    place_ref,
    bucket_ref,
    x_in,
    inv_in,
    pool_in,
    mix_in,
    stat_in,
    zed_in,
    dx_in,
    mean_in,
    flat_ref,
    vec_ref,
    payload_hbm,
    vector_ref,
    payload_ref,
    image_ref,
    col_ref,
    dx_ref,
    back_ref,
    acc_ref,
    sem,
):
    pair = pl.program_id(0) if pairs > 1 else 0
    x_ref, inv_ref, pool_ref, mix_ref, stat_ref, zed_ref, low_ref, mean_ref = (
        ref.at[0] for ref in (x_in, inv_in, pool_in, mix_in, stat_in, zed_in, dx_in, mean_in)
    )
    bucket_of = bucket_reader(place_ref, bucket_ref, strip_count)
    shape = Geometry(bucket_of, pair)
    count_two = shape.count_two
    gain1, bias1, scale1, gain2 = (vec_ref[n : n + 1] for n in range(4))
    mean1, scaling1, mean2, scaling2 = (stat_ref[n] for n in range(4))
    normal2 = (scaling2, -mean2 * scaling2)
    clear_edges(col_ref)
    nothing = jnp.zeros((8, C2), f32)
    back_gain2 = scaling2 * gain2
    back_mean2 = -scaling2 * mean_ref[0]
    back_normal2 = scaling2 * mean_ref[1]

    if pairs > 1:

        @pl.when(pair == 0)
        def _():
            acc_ref[...] = jnp.zeros(acc_ref.shape, f32)

    def add_up(n, total):
        acc_ref[n] = total if pairs == 1 else acc_ref[n] + total

    def unmix(k, d_scale):
        rows = step_rows(k)
        for pr in range(2):
            weighted = []
            for pc in range(2):
                plane = pr * 2 + pc
                share = inv_ref[plane, rows]
                normal = affine(mix_ref[plane, rows], *normal2)
                back = affine(low_ref[plane, rows], back_gain2, back_mean2)
                back = back - scaled(normal, back_normal2)
                d_mixed = jnp.where(share > 0.0, zed_ref[plane, rows] + back, 0.0)
                dx_ref[plane, rows] = d_mixed
                d_scale = d_scale + fold(pool_ref[plane, rows] * d_mixed)
                weighted.append(scale1 * d_mixed * share)
            put_col_windows(col_ref, pr, k, *weighted)
        return d_scale

    add_up(2, sweep(unmix, nothing))
    normal1 = (spread(scaling1, C2), spread(-mean1 * scaling1, C2))

    def unpool(k, carry):
        d_shift, d_gain = carry
        rows = step_rows(k)
        for pc in range(2):
            windows = row_windows(col_ref, pc, k)
            for pr in range(2):
                plane = pr * 2 + pc
                valid = inv_ref[plane, rows] > 0.0
                d_normal = windows[pr] - scale1 * dx_ref[plane, rows]
                d_normal = jnp.where(valid, d_normal, 0.0)
                back_ref[plane, rows] = d_normal
                normal = affine(x_ref[plane, rows], *normal1)
                d_shift = d_shift + fold(d_normal)
                d_gain = d_gain + fold(d_normal * normal)
        return (d_shift, d_gain)

    d_shift, d_gain = sweep(unpool, (nothing, nothing))
    add_up(1, d_shift)
    add_up(0, d_gain)
    mean_shift = by_image(d_shift * gain1) / count_two
    mean_gain = by_image(d_gain * gain1) / count_two
    back_gain1 = scaling1 * gain1
    back_mean1 = spread(-scaling1 * mean_shift, C2)
    back_normal1 = spread(scaling1 * mean_gain, C2)

    def unnorm(k, carry):
        rows = step_rows(k)
        for plane in range(4):
            normal = affine(x_ref[plane, rows], *normal1)
            back = affine(back_ref[plane, rows], back_gain1, back_mean1)
            back = back - scaled(normal, back_normal1)
            valid = inv_ref[plane, rows] > 0.0
            dx_ref[plane, rows] = jnp.where(valid, dx_ref[plane, rows] + back, 0.0)
        return carry

    sweep(unnorm, 0)

    def give_back(plane, here, spot, there):
        image_ref[spot, there] = dx_ref[plane, here]

    image_ref[...] = jnp.zeros(image_ref.shape, f32)
    each_image(bucket_of, pair, give_back)

    for spot in range(2 * STRIPS):
        target = strip_place(pair, spot, strip_count)
        for within in range(SR):
            rows = slice(within * CW, within * CW + CW)
            payload_ref[target, within] = image_ref[spot, rows].astype(bf16)

    def finish():
        copy = pltpu.make_async_copy(payload_ref, payload_hbm, sem)
        copy.start()
        vector_ref[...] = flat_ref[...]
        for n in range(3):
            vector_ref[n : n + 1] = jnp.sum(acc_ref[n], axis=0, keepdims=True)
        copy.wait()

    if pairs == 1:
        finish()
    else:
        pl.when(pair == pairs - 1)(finish)


def run_exit(place, buckets, state, back, flat, vec, strip_count):
    pairs = strip_count // 8
    payload = (strip_count, SR, CW, C2)
    make = pltpu.VMEM if pairs == 1 else jax.ShapeDtypeStruct
    plane_f32 = pltpu.VMEM((4, AREA, C2), f32)
    arrays = [*state, *back]
    if pairs == 1:
        arrays = held_in(pltpu.VMEM, *arrays)
    return pl.pallas_call(
        functools.partial(exit_kernel, pairs, strip_count),
        grid=() if pairs == 1 else (pairs,),
        in_specs=[SMEM] * 2
        + pair_specs(pairs, STATE + BACK, pl.Buffered(1))
        + whole_specs(pairs, [flat.shape, vec.shape]),
        out_specs=[HBM] + whole_specs(pairs, [flat.shape]),
        out_shape=[pltpu.HBM(payload, bf16), make(flat.shape, f32)],
        scratch_shapes=[
            pltpu.VMEM(payload, bf16),
            pltpu.VMEM((2 * STRIPS, STRIP_ROWS, C2), f32),
            pltpu.VMEM((4, AREA + 2 * LINE, C2), f32),
            plane_f32,
            plane_f32,
            pltpu.VMEM((3, 8, C2), f32),
            pltpu.SemaphoreType.DMA,
        ],
        compiler_params=roomy(8 if pairs == 1 else 40),
        name="exit",
    )(place, buckets, *arrays, flat, vec)


def dense_blocks(values):
    return jnp.concatenate([values[:, :HALF], values[:, HALF:]], axis=2).astype(bf16)


def pack_kernel(master_ref, dense_ref):
    dense_ref[...] = dense_blocks(master_ref[...])


def pack(master):
    owned = master.shape[0]
    return pl.pallas_call(
        pack_kernel,
        out_shape=jax.ShapeDtypeStruct((owned, HALF, 2 * BS), bf16),
        name="pack",
    )(master)


def pack_pieces_kernel(place_ref, master_hbm, pixel_hbm, *refs):
    out_refs, (wide_ref, master_ref, pixel_ref, sem) = refs[:-4], refs[-4:]
    owned = master_ref.shape[0]
    slots = pixel_ref.shape[2]
    copies = [pltpu.make_async_copy(pixel_hbm, pixel_ref, sem.at[0])]
    parts = [(0, owned // 2), (owned // 2, owned - owned // 2)]
    for n, part in enumerate(parts):
        copies.append(
            pltpu.make_async_copy(
                master_hbm.at[pl.ds(*part)], master_ref.at[pl.ds(*part)], sem.at[1 + n]
            )
        )
    for copy in copies:
        copy.start()
    copies[0].wait()

    def widen_row(row, carry):
        start = pl.multiple_of(row * CW * slots, 8)
        values = pixel_ref[row].astype(f32).reshape(CW * slots, C2)
        wide_ref[pl.ds(start, CW * slots)] = values
        return carry

    lax.fori_loop(0, SR, widen_row, 0)
    for k, ref in enumerate(out_refs):
        for other in range(2):
            slot = place_ref[0] ^ (2 * k + other)
            first = other * (ref.shape[0] - STRIP_ROWS)
            strip = wide_ref[pl.ds(slot, STRIP_ROWS, stride=slots)]
            ref[first : first + STRIP_ROWS] = strip.astype(bf16)
    for (first, count), copy in zip(parts, copies[1:]):
        copy.wait()
        dense = dense_blocks(master_ref[first : first + count]).reshape(count * HALF, 2 * BS)
        start = STRIP_ROWS + first * HALF
        for ref in out_refs[:3]:
            ref[start : start + count * HALF] = dense


def pack_pieces(place, master, pixels):
    slots = pixels.shape[2]
    rows = master.shape[0] * HALF
    shapes = [(rows + 2 * STRIP_ROWS, 2 * BS)] * 3 + [(2 * STRIP_ROWS, 2 * BS)]
    return pl.pallas_call(
        pack_pieces_kernel,
        in_specs=[SMEM] + [HBM] * 2,
        out_specs=[VMEM_BLOCK] * 4,
        out_shape=[pltpu.VMEM(shape, bf16) for shape in shapes],
        scratch_shapes=[
            pltpu.VMEM((STRIP_ROWS * slots, C2), f32),
            pltpu.VMEM(master.shape, f32),
            pltpu.VMEM(pixels.shape, bf16),
            pltpu.SemaphoreType.DMA((3,)),
        ],
        compiler_params=roomy(12),
        name="pack",
    )(place, *held_in(pltpu.HBM, master, pixels))


def fold_pair_kernel(near_ref, got_ref, own_ref, *part_refs):
    share = own_ref.shape[0]

    def one(n, carry):
        own_ref[n] = near_ref[n].astype(f32) + got_ref[n].astype(f32)
        for k, ref in enumerate(part_refs):
            here = (k + 1) * share + n
            ref[n] = near_ref[here] + got_ref[here]
        return carry

    lax.fori_loop(0, share, one, 0, unroll=4)


def fold_pair(near, got, groups):
    shape = ((near.shape[0] - 1) // groups,) + near.shape[1:]
    return pl.pallas_call(
        fold_pair_kernel,
        in_specs=[VMEM_BLOCK] * 2,
        out_specs=[VMEM_BLOCK] * groups,
        out_shape=[pltpu.VMEM(shape, f32)] + [pltpu.VMEM(shape, bf16)] * (groups - 1),
        compiler_params=roomy(4),
        name="fold_pair",
    )(*held_in(pltpu.VMEM, near, got))


def fold_tile_kernel(pieces, spot_ref, *refs):
    piece_refs, refs = refs[:pieces], refs[pieces:]
    vector_refs, refs = refs[:pieces], refs[pieces:]
    out_refs, sum_ref = refs[:-1], refs[-1]
    groups = len(out_refs)
    share = out_refs[0].shape[0]
    owned = piece_refs[0].shape[0]
    total = vector_refs[0][...]
    for ref in vector_refs[1:]:
        total = total + ref[...]
    for n in range(sum_ref.shape[0]):
        sum_ref[n] = jnp.zeros((HALF, 128), f32)
    for n in range(VEC_BLOCKS):
        sum_ref[n] = total[n * HALF : (n + 1) * HALF]

    def one(n, carry):
        for k, out_ref in enumerate(out_refs):
            number = lax.rem(spot_ref[0] + k, groups) * share + n
            block = jnp.minimum(number, owned - 1)
            total = piece_refs[0][block].astype(f32)
            for ref in piece_refs[1:]:
                total = total + ref[block].astype(f32)
            rest = sum_ref[jnp.maximum(number - owned, 0)]
            out_ref[n] = jnp.where(number < owned, total, rest).astype(out_ref.dtype)
        return carry

    lax.fori_loop(0, share, one, 0, unroll=share <= 16)


def fold_tile(spot, pieces, vectors, extra, groups):
    shape = ((pieces[0].shape[0] + extra) // groups,) + pieces[0].shape[1:]
    return pl.pallas_call(
        functools.partial(fold_tile_kernel, len(pieces)),
        in_specs=[SMEM] + [VMEM_BLOCK] * (len(pieces) + len(vectors)),
        out_specs=[VMEM_BLOCK] * groups,
        out_shape=[pltpu.VMEM(shape, f32)] + [pltpu.VMEM(shape, bf16)] * (groups - 1),
        scratch_shapes=[pltpu.VMEM((extra, HALF, 128), f32)],
        compiler_params=roomy(8),
        name="fold_tile",
    )(spot, *held_in(pltpu.VMEM, *pieces, *vectors))


def fold_batch_kernel(owned, vector_weight, spot_ref, *refs):
    part_refs, (total_ref, norm_ref) = refs[:-2], refs[-2:]
    share = total_ref.shape[0]
    square = jnp.zeros((8, 128), f32)
    for n in range(share):
        total = part_refs[0][n].astype(f32)
        for ref in part_refs[1:]:
            total = total + ref[n].astype(f32)
        total_ref[n] = total.astype(bf16)
        weight = jnp.where(spot_ref[0] * share + n < owned, 1.0, vector_weight)
        square = square + weight * fold(total * total)
    square = jnp.sum(jnp.sum(square, axis=1, keepdims=True), axis=0, keepdims=True)
    norm_ref[...] = jnp.broadcast_to(square[None], norm_ref.shape)


def fold_batch(spot, parts, owned, tile_count):
    count = tile_count * len(parts)
    return pl.pallas_call(
        functools.partial(fold_batch_kernel, owned, 1.0 / tile_count),
        in_specs=[SMEM] + [VMEM_BLOCK] * len(parts),
        out_specs=[VMEM_BLOCK] * 2,
        out_shape=[pltpu.VMEM(parts[0].shape, bf16), pltpu.VMEM((count, 1, 128), f32)],
        name="fold_batch",
    )(spot, *held_in(pltpu.VMEM, *parts))


def update_kernel(owned, groups, spot_ref, norm_ref, *refs):
    quarters, refs = refs[:groups], refs[groups:]
    stat_hbm, out_hbm, (vector_ref, clip_ref), refs = refs[:5], refs[5:10], refs[10:12], refs[12:]
    stat_refs, out_refs, (in_sem, out_sem) = refs[:5], refs[5:10], refs[10:]
    master_ref, left_stat_ref, right_stat_ref, left_root_ref, right_root_ref = stat_refs
    grad_ref, left_ref, right_ref, new_ref, copy_ref = out_refs
    share = quarters[0].shape[0]
    spans = spans_of(owned)

    def copies_of(sources, targets, sems):
        return [
            [
                pltpu.make_async_copy(
                    source.at[pl.ds(*span)], target.at[pl.ds(*span)], sems.at[5 * n + k]
                )
                for k, (source, target) in enumerate(zip(sources, targets))
            ]
            for n, span in enumerate(spans)
        ]

    copies_in = copies_of(stat_hbm, stat_refs, in_sem)
    copies_out = copies_of(out_refs, out_hbm, out_sem)
    for copies in copies_in:
        for copy in copies:
            copy.start()
    norm = jnp.sqrt(jnp.sum(norm_ref[...], axis=0))
    factor = jnp.minimum(1.0, clip_limit / norm)
    left_half = lax.broadcasted_iota(jnp.int32, (HALF, 128), 1) < BS

    def summed(number):
        source = number // share
        local = number - source * share
        turn = lax.rem(spot_ref[0] - source + groups, groups)
        value = quarters[0][local].astype(f32)
        for k in range(1, groups):
            value = jnp.where(turn == k, quarters[k][local].astype(f32), value)
        return value * factor

    def side_by_side(first, count):
        sides = []
        for n in range(first, first + count, 2):
            dense = summed(n)
            turned = pltpu.roll(dense, BS, 1)
            if n + 1 < first + count:
                second = summed(n + 1)
                top = jnp.where(left_half, dense, pltpu.roll(second, BS, 1))
                low = jnp.where(left_half, turned, second)
                side = jnp.concatenate([top, low], axis=0)
                grad_ref[n + 1] = pltpu.roll(side, BS, 1)[:, :BS]
            else:
                side = jnp.concatenate([dense, turned], axis=0)[:, :BS]
            grad_ref[n] = side[:, :BS]
            sides.append(side.astype(bf16))
        return jnp.concatenate(sides, axis=1)

    def diagonal_of(count):
        order = (count * BS, count * BS)
        return lax.broadcasted_iota(jnp.int32, order, 0) // BS == (
            lax.broadcasted_iota(jnp.int32, order, 1) // BS
        )

    clip_ref[...] = norm
    for n in range(vector_ref.shape[0]):
        vector_ref[n] = summed(owned + n)
    for (first, length), arriving, leaving in zip(spans, copies_in, copies_out):
        parts = [(n, min(4, first + length - n)) for n in range(first, first + length, 4)]
        wides = [side_by_side(*part) for part in parts]
        tall = [
            jnp.where(diagonal_of(count), jnp.concatenate([wide] * count, axis=0), 0.0)
            for (_, count), wide in zip(parts, wides)
        ]
        lefts = [product_nt(one, wide) for one, wide in zip(tall, wides)]
        rights = [product_tn(wide, wide) for wide in wides]
        for copy in arriving:
            copy.wait()
        stepped = []
        for (start, count), wide in zip(parts, wides):
            roots = left_root_ref[pl.ds(start, count)].reshape(count * BS, BS).astype(bf16)
            stepped.append(product(roots, wide))
        for (start, count), left, right in zip(parts, lefts, rights):
            here = pl.ds(start, count)
            left_ref[here] = 0.5 * left_stat_ref[here] + 0.5 * left.reshape(count, BS, BS)
            for n in range(count):
                at = n // 2 * 128
                block = right[n * BS : n * BS + BS, at : min(at + 128, count * BS)]
                if n % 2:
                    block = pltpu.roll(block, BS, 1)
                right_ref[start + n] = 0.5 * right_stat_ref[start + n] + 0.5 * block[:, :BS]
        for (start, count), value in zip(parts, stepped):
            here = pl.ds(start, count)
            value = jnp.where(diagonal_of(count), value, 0.0).astype(bf16)
            roots = right_root_ref[here].reshape(count * BS, BS).astype(bf16)
            value = product(value, roots).reshape(count, BS, BS)
            new = master_ref[here] - rate_matrix * value
            new_ref[here] = new
            copy_ref[here] = new.astype(bf16)
        for copy in leaving:
            copy.start()
    for leaving in copies_out:
        for copy in leaving:
            copy.wait()


def spans_of(owned):
    spans = []
    first = 0
    while first < owned:
        length = min(8 if first == 0 else 12, owned - first)
        spans.append((first, length))
        first += length
    return spans


def update(spot, norm, quarters, extra, *stats):
    shape = stats[0].shape
    groups = len(quarters)
    types = [f32] * 4 + [bf16]
    steps = len(spans_of(shape[0]))
    return pl.pallas_call(
        functools.partial(update_kernel, shape[0], groups),
        in_specs=[SMEM] + [VMEM_BLOCK] * (groups + 1) + [HBM] * 5,
        out_specs=[HBM] * 5 + [VMEM_BLOCK] * 2,
        out_shape=[pltpu.HBM(shape, kind) for kind in types]
        + [
            pltpu.VMEM((extra, HALF, 128), f32),
            pltpu.VMEM((1, 128), f32),
        ],
        scratch_shapes=[pltpu.VMEM(shape, f32)] * 5
        + [pltpu.VMEM(shape, kind) for kind in types]
        + [
            pltpu.SemaphoreType.DMA((5 * steps,)),
            pltpu.SemaphoreType.DMA((5 * steps,)),
        ],
        compiler_params=roomy(20),
        name="update",
    )(spot, *held_in(pltpu.VMEM, norm, *quarters), *held_in(pltpu.HBM, *stats))


def share_out(pieces, axis):
    return lax.all_to_all(pieces, axis, split_axis=0, concat_axis=0, tiled=True)


def swap(piece, distance):
    count = lax.axis_size("tile")
    return lax.ppermute(piece, "tile", [(i, i ^ distance) for i in range(count)])


def on_device(
    pixels,
    buckets,
    slot_owner_table,
    out_grad,
    master,
    left_stat,
    right_stat,
    left_root,
    right_root,
    vectors,
    moment,
):
    tile_count = lax.axis_size("tile")
    tile_place = lax.axis_index("tile")
    slot_count = pixels.shape[2]
    group_count = tile_count // STRIPS
    pairs = group_count // 2
    owned = master.shape[0]
    slots = owned * tile_count
    batch_count = lax.axis_size("batch")
    spot = lax.axis_index("batch").astype(jnp.int32).reshape(1)
    extra = extra_of(owned, batch_count)
    place = tile_place.astype(jnp.int32).reshape(1)
    paired = tile_count == 8
    numbers = jnp.arange(slots, dtype=jnp.int32)
    slot_of = jnp.sum(
        jnp.where(slot_owner_table[None, :] == numbers[:, None], numbers[None, :], 0), axis=1
    )
    if paired:
        owner = slot_of // owned
        apart = owner ^ tile_place
        apart = (apart & 1) * (tile_count // 2) + (apart >> 1)
        slot_of = slot_of + owned * (apart - owner)
    half = slots // 2
    near_place = jnp.where(slot_of < half, slot_of, half)
    far_place = jnp.where(slot_of < half, half, slot_of - half)
    vec = vectors.reshape(-1, 128)
    turned = lax.dynamic_index_in_dim(
        buckets.reshape(group_count, slot_count), tile_place, 1, keepdims=False
    ) >= 2
    flips = turned.reshape(-1, 1, 1, 1)
    goal = out_grad.reshape(2 * pairs, H3, W3, C3)
    goal = jnp.where(flips, goal.transpose(0, 2, 1, 3), goal)[:, :LINES]
    goal = goal.reshape(pairs, 2, LINES, W3, C3).transpose(0, 2, 3, 1, 4)
    goal = goal.reshape(pairs, LINES, 2 * W3, C3)
    goal = jnp.pad(goal, ((0, 0), (0, 0), (0, LINE - 2 * W3), (0, WIDE - C3)))
    goal = goal.reshape(pairs, AREA, WIDE)

    if paired:
        own, for_x, for_y, for_both = pack_pieces(
            place, master, pixels[0, 0].transpose(1, 2, 0, 3)
        )
        goal, vec, slot_of, near_place, far_place, for_both = lax.optimization_barrier(
            (goal, vec, slot_of, near_place, far_place, for_both)
        )
        from_x, from_y, strips_both = swap(for_x, 2), swap(for_y, 4), swap(for_both, 6)
        near_half = (owned + 1) // 2
        middle = STRIP_ROWS + near_half * HALF
        first_half = swap(from_x[STRIP_ROWS:middle], 4)
        second_half = swap(from_y[middle : STRIP_ROWS + owned * HALF], 2)
        mine = [own, from_x, from_y, strips_both, first_half, second_half]
        both = mine + [swap(piece, 1) for piece in mine]
        strips = both[:4] + both[6:10]
        pieces = [both[n] for n in (0, 1, 2, 4, 5, 6, 7, 8, 10, 11)]
        spans = [(STRIP_ROWS, owned)] * 3 + [(0, near_half), (0, owned - near_half)]
        spans = spans * 2
    else:
        pieces = [lax.all_gather(pack(master), "tile", axis=0, tiled=True).reshape(-1, 2 * BS)]
        spans = [(0, slots)]
        strips = share_out(pixels.reshape(tile_count, STRIP, C2), "tile")
        strips = [jnp.pad(strips, ((0, 0), (0, STRIP_ROWS - STRIP), (0, 0)))]

    weights = run_unpack(slot_of, pieces, spans)
    state = run_entry(place, buckets, strips, vec, tile_count)
    result, *back, near, far, flat = run_main(
        (near_place, far_place),
        place,
        buckets,
        state,
        goal,
        vec,
        weights,
        tile_count,
    )
    pixel_back, vector = run_exit(place, buckets, state, back, flat, vec, tile_count)
    if paired:
        own, *parts = fold_pair(near, swap(far, 1), tile_count // 2)
        pieces = [own] + [swap(part, 2 * k + 2) for k, part in enumerate(parts)]
        vector, _ = lax.optimization_barrier((vector, parts[0]))
        vector = vector + swap(vector, 1)
        vectors_in = [vector] + [swap(vector, 2 * k) for k in range(1, tile_count // 2)]
    else:
        outgoing = jnp.concatenate([near[:half], far[:half]], axis=0)
        pieces = list(share_out(outgoing.reshape(tile_count, owned, HALF, 128), "tile"))
        vectors_in = list(lax.all_gather(vector, "tile"))
    result, pieces[1] = lax.optimization_barrier((result, pieces[1]))
    result = result.reshape(pairs, LINES, LINE, WIDE)[:, :, : 2 * W3, :C3]
    result = result.reshape(pairs, LINES, W3, 2, C3).transpose(0, 3, 1, 2, 4)
    result = result.reshape(2 * pairs, LINES, W3, C3)
    result = jnp.pad(result, ((0, 0), (0, H3 - LINES), (0, 0), (0, 0)))
    result = jnp.where(flips, result.transpose(0, 2, 1, 3), result)
    result = result.reshape(out_grad.shape)
    result = with_layout_constraint(result, Layout(major_to_minor=(0, 1, 2, 4, 5, 3, 6)))
    result, vectors_in[0] = lax.optimization_barrier((result, vectors_in[0]))
    own, *parts = fold_tile(spot, pieces, vectors_in, extra, batch_count)
    pixel_back, parts[0] = lax.optimization_barrier((pixel_back, parts[0]))
    returned = share_out(pixel_back, "tile")
    parts = [
        lax.ppermute(part, "batch", [(i, (i + k + 1) % batch_count) for i in range(batch_count)])
        for k, part in enumerate(parts)
    ]
    quarter, norm = fold_batch(spot, [own] + parts, owned, tile_count)
    returned, norm = lax.optimization_barrier((returned, norm))
    norm = share_out(norm, ("batch", "tile"))
    returned = returned.astype(f32).reshape(pixels.shape)
    returned = with_layout_constraint(returned, Layout(major_to_minor=(0, 1, 3, 4, 2, 5)))
    returned, norm = lax.optimization_barrier((returned, norm))
    quarters = [quarter] + [
        lax.ppermute(quarter, "batch", [(i, (i + k) % batch_count) for i in range(batch_count)])
        for k in range(1, batch_count)
    ]
    block_grad, left_new, right_new, master_new, weight_copy, whole_vector, clip = update(
        spot, norm, quarters, extra, master, left_stat, right_stat, left_root, right_root
    )
    clip_norm = clip[0, 0]
    share = vectors.shape[0] // tile_count
    whole_vector = whole_vector.reshape(-1)
    vec_grad = lax.dynamic_slice_in_dim(whole_vector, tile_place * share, share, 0)
    vec_moment = moment + vec_grad * vec_grad
    own_vectors = lax.dynamic_slice_in_dim(vectors, tile_place * share, share, 0)
    vec_new = own_vectors - rate_vector * vec_grad / (jnp.sqrt(vec_moment) + eps_adagrad)
    return (
        result,
        returned,
        clip_norm,
        block_grad,
        left_new,
        right_new,
        master_new,
        weight_copy,
        vec_grad,
        vec_moment,
        vec_new,
    )


def solution(mesh):
    placed = (
        P("batch", "tile", None, None, None, None),
        P("batch"),
        P(),
        P("batch", "tile", None, None, None, None, None),
        P("tile", None, None),
        P("tile", None, None),
        P("tile", None, None),
        P("tile", None, None),
        P("tile", None, None),
        P(),
        P("tile"),
    )
    return jax.shard_map(
        on_device,
        mesh=mesh,
        in_specs=placed,
        out_specs=(
            P("batch", "tile", None, None, None, None, None),
            P("batch", "tile", None, None, None, None),
            P(),
            P("tile", None, None),
            P("tile", None, None),
            P("tile", None, None),
            P("tile", None, None),
            P("tile", None, None),
            P("tile"),
            P("tile"),
            P("tile"),
        ),
        check_vma=False,
    )
```

profile of v0, /device:TPU:0, one launch (start us, length us, event | category | flops | bytes accessed | tf_op | source)
XLA Modules:
  0.0 117.4 jit_solution(4197543126634792019)
XLA Ops:
  0.7 1.9 %pack.1 = (bf16[1984,128]{1,0:T(8,128)(2,1)S(1)}, bf16[1984,128]{1,0:T(8,128)(2,1)S(1)}, bf16[1984,128]{1,0:T(8,128)(2,1)S(1)}, bf16[672,128]{1,0:T(8,128)(2,1)S(1)}) custom-call(s32[1]{0:T(128)} %bitcast.6.place_ref, f32[41,64,64]{2,1,0:T(8,128)} %refs_4_.1, bf16[9,36,8,128]{3,2,1,0:T(8,128)(2,1)} %bitcast.45), custom_call_target="tpu_custom_call" | custom-call | tf_op jit(solution)/shard_map/pack/pallas_call | solution.py:1191
  2.6 3.0 %collective-permute-start = (bf16[1984,128]{1,0:T(8,128)(2,1)S(1)}, bf16[1984,128]{1,0:T(8,128)(2,1)S(1)}, u32[]{:S(2)}, u32[]{:S(2)}) collective-permute-start(bf16[1984,128]{1,0:T(8,128)(2,1)S(1)} %get-tuple-element.73), channel_id=1, source_target_pairs={{0,2},{1,3},{2,0},{3,1},{4,6},{5,7},{6,4},{7,5},{8,10},{9,11},{10,... | collective-permute-start | bytes 1523720 | tf_op jit(solution)/shard_map/ppermute | solution.py:1444
  5.6 1.5 %collective-permute-start.1 = (bf16[1984,128]{1,0:T(8,128)(2,1)S(1)}, bf16[1984,128]{1,0:T(8,128)(2,1)S(1)}, u32[]{:S(2)}, u32[]{:S(2)}) collective-permute-start(bf16[1984,128]{1,0:T(8,128)(2,1)S(1)} %get-tuple-element.74), channel_id=1, source_target_pairs={{0,4},{1,5},{2,6},{3,7},{4,0},{5,1},{6,2},{7,3},{8,12},{9,13},{10,... | collective-permute-start | bytes 1523720 | tf_op jit(solution)/shard_map/ppermute | solution.py:1444
  7.4 1.2 %fusion.1 = bf16[1,14,18,2,320]{4,3,2,1,0:T(2,128)(2,1)} fusion(bf16[2,18,18,320]{3,0,2,1:T(2,128)(2,1)S(1)} %bitcast.43, pred[2]{0:T(512)(128)(4,1)S(1)} %compare_reduce_fusion, bf16[2,18,18,320]{3,0,1,2:T(2,128)(2,1)S(1)} %bitcast.44), kind=kLoop, calls=%fused_computation.7 | loop fusion | flops 161280 | bytes 1097216 | tf_op jit(solution)/shard_map/transpose | solution.py:1491
  8.6 1.3 %reshape.79 = bf16[1,14,36,320]{3,2,1,0:T(8,128)(2,1)S(1)} reshape(bf16[1,14,18,2,320]{4,3,2,1,0:T(2,128)(2,1)} %fusion.1) | data formatting | bytes 645120 | tf_op jit(solution)/shard_map/reshape | solution.py:1492
  10.3 7.6 %collective-permute-done.refs_1_ = bf16[1984,128]{1,0:T(8,128)(2,1)S(1)} collective-permute-done((bf16[1984,128]{1,0:T(8,128)(2,1)S(1)}, bf16[1984,128]{1,0:T(8,128)(2,1)S(1)}, u32[]{:S(2)}, u32[]{:S(2)}) %collective-permute-start) | collective-permute-done | bytes 507936 | tf_op jit(solution)/shard_map/ppermute | solution.py:1444
  18.0 4.3 %collective-permute-done.1.refs_2_ = bf16[1984,128]{1,0:T(8,128)(2,1)S(1)} collective-permute-done((bf16[1984,128]{1,0:T(8,128)(2,1)S(1)}, bf16[1984,128]{1,0:T(8,128)(2,1)S(1)}, u32[]{:S(2)}, u32[]{:S(2)}) %collective-permute-start.1) | collective-permute-done | bytes 507936 | tf_op jit(solution)/shard_map/ppermute | solution.py:1444
  22.3 0.5 collective-permute-start.6
  22.8 1.6 %collective-permute-start.7 = (bf16[672,128]{1,0:T(8,128)(2,1)S(1)}, bf16[672,128]{1,0:T(8,128)(2,1)S(1)}, u32[]{:S(2)}, u32[]{:S(2)}) collective-permute-start(bf16[672,128]{1,0:T(8,128)(2,1)S(1)} %slice.22), channel_id=1, source_target_pairs={{0,4},{1,5},{2,6},{3,7},{4,0},{5,1},{6,2},{7,3},{8,12},{9,13},{10,... | collective-permute-start | bytes 516104 | tf_op jit(solution)/shard_map/ppermute | solution.py:1444
  24.4 0.6 collective-permute-start.8
  25.0 4.1 %collective-permute-done.7.refs_3_ = bf16[672,128]{1,0:T(8,128)(2,1)S(1)} collective-permute-done((bf16[672,128]{1,0:T(8,128)(2,1)S(1)}, bf16[672,128]{1,0:T(8,128)(2,1)S(1)}, u32[]{:S(2)}, u32[]{:S(2)}) %collective-permute-start.7) | collective-permute-done | bytes 172064 | tf_op jit(solution)/shard_map/ppermute | solution.py:1444
  29.2 1.5 %collective-permute-done.8.refs_4_ = bf16[640,128]{1,0:T(8,128)(2,1)S(1)} collective-permute-done((bf16[640,128]{1,0:T(8,128)(2,1)S(1)}, bf16[640,128]{1,0:T(8,128)(2,1)S(1)}, u32[]{:S(2)}, u32[]{:S(2)}) %collective-permute-start.8) | collective-permute-done | bytes 163872 | tf_op jit(solution)/shard_map/ppermute | solution.py:1444
  30.7 2.7 %entry.1 = (f32[1,4,560,128]{3,2,1,0:T(8,128)S(1)}, f32[1,4,560,128]{3,2,1,0:T(8,128)S(1)}, f32[1,4,560,128]{3,2,1,0:T(8,128)S(1)}, f32[1,4,560,128]{3,2,1,0:T(8,128)S(1)}, f32[1,4,8,128]{3,2,1,0:T(8,128)S(1)}) custom-call(s32[1]{0:T(128)} %bitcast.6.place_ref, s32[16]{0:T(128)S(1)} %copy-done.1, f32[41,128]{1,0:T(8,128)S(1)} %bitcast.36, ...), custom_call_target="tpu_custom_call" | custom-call | tf_op jit(solution)/shard_map/entry/pallas_call | solution.py:385
  33.4 1.5 %unpack.1 = (bf16[128,512]{1,0:T(8,128)(2,1)S(1)}, bf16[512,128]{1,0:T(8,128)(2,1)S(1)}, bf16[1152,384]{1,0:T(8,128)(2,1)S(1)}, bf16[384,1280]{1,0:T(8,128)(2,1)S(1)}, bf16[1280,384]{1,0:T(8,128)(2,1)S(1)}) custom-call(s32[328]{0:T(512)S(1)} %get-tuple-element.80.slot_ref, bf16[1984,128]{1,0:T(8,128)(2,1)S(1)} %get-tuple-element.72.refs_0_, ...), custom_call_target="tpu_custom_call" | custom-call | tf_op jit(solution)/shard_map/unpack/pallas_call | solution.py:436
  34.9 20.7 %blocks.1 = (f32[1,560,384]{2,1,0:T(8,128)S(1)}, f32[1,4,560,128]{3,2,1,0:T(8,128)S(1)}, f32[1,4,560,128]{3,2,1,0:T(8,128)S(1)}, f32[1,2,8,128]{3,2,1,0:T(8,128)...) custom-call(s32[328]{0:T(512)S(1)} %compare_select_fusion.1.near_place, ...), custom_call_target="tpu_custom_call" | custom-call | tf_op jit(solution)/shard_map/blocks/pallas_call | solution.py:952
  55.6 0.6 collective-permute-start.11
  56.2 2.7 %collective-permute-done.11.got_ref = bf16[165,32,128]{2,1,0:T(8,128)(2,1)S(1)} collective-permute-done((bf16[165,32,128]{2,1,0:T(8,128)(2,1)S(1)}, bf16[165,32,128]{2,1,0:T(8,128)(2,1)S(1)}, u32[]{:S(2)}, u32[]{:S(2)}) %collective-permute-start.11) | collective-permute-done | bytes 1351712 | tf_op jit(solution)/shard_map/ppermute | solution.py:1444
  58.9 1.0 fold_pair.1
  59.9 0.5 collective-permute-start.12
  60.4 1.6 %collective-permute-start.14 = (bf16[41,32,128]{2,1,0:T(8,128)(2,1)S(1)}, bf16[41,32,128]{2,1,0:T(8,128)(2,1)S(1)}, u32[]{:S(2)}, u32[]{:S(2)}) collective-permute-start(bf16[41,32,128]{2,1,0:T(8,128)(2,1)S(1)} %get-tuple-element.103), channel_id=1, source_target_pairs={{0,4},{1,5},{2,6},{3,7},{4,0},{5,1},{6,2},{7,3},{8,12},{9,13},{10,... | collective-permute-start | bytes 1007624 | tf_op jit(solution)/shard_map/ppermute | solution.py:1444
  62.0 1.4 %collective-permute-start.15 = (bf16[41,32,128]{2,1,0:T(8,128)(2,1)S(1)}, bf16[41,32,128]{2,1,0:T(8,128)(2,1)S(1)}, u32[]{:S(2)}, u32[]{:S(2)}) collective-permute-start(bf16[41,32,128]{2,1,0:T(8,128)(2,1)S(1)} %get-tuple-element.104), channel_id=1, source_target_pairs={{0,6},{1,7},{2,4},{3,5},{4,2},{5,3},{6,0},{7,1},{8,14},{9,15},{10,... | collective-permute-start | bytes 1007624 | tf_op jit(solution)/shard_map/ppermute | solution.py:1444
  63.4 3.8 %exit.1 = (bf16[8,9,36,128]{3,2,1,0:T(8,128)(2,1)}, f32[64,128]{1,0:T(8,128)S(1)}) custom-call(s32[1]{0:T(128)} %bitcast.6.place_ref, s32[16]{0:T(128)S(1)} %copy-done.1, f32[1,4,560,128]{3,2,1,0:T(8,128)S(1)} %get-tuple-element.91.x_in, f32[1,4,560,128]{3,2,1,0:T(8,128)S(1)} %get-tuple-element.76.inv_in, f32[1,4,560,128]{3,2,1,0:T(8,128)S(1)} %get-tuple-element.92.pool_in, ...), custom_call_target="tpu_custom_call" | custom-call | tf_op jit(solution)/shard_map/exit/pallas_call | solution.py:1111
  67.3 1.2 %collective-permute-done.13 = f32[64,128]{1,0:T(8,128)S(1)} collective-permute-done((f32[64,128]{1,0:T(8,128)S(1)}, f32[64,128]{1,0:T(8,128)S(1)}, u32[]{:S(2)}, u32[]{:S(2)}) %collective-permute-start.13) | collective-permute-done | bytes 32800 | tf_op jit(solution)/shard_map/ppermute | solution.py:1444
  68.5 0.5 collective-permute-start.16
  69.0 1.7 %collective-permute-start.17 = (f32[64,128]{1,0:T(8,128)S(1)}, f32[64,128]{1,0:T(8,128)S(1)}, u32[]{:S(2)}, u32[]{:S(2)}) collective-permute-start(f32[64,128]{1,0:T(8,128)S(1)} %add.37.refs_4_), channel_id=1, source_target_pairs={{0,4},{1,5},{2,6},{3,7},{4,0},{5,1},{6,2},{7,3},{8,12},{9,13},{10,... | collective-permute-start | bytes 98312 | tf_op jit(solution)/shard_map/ppermute | solution.py:1444
  70.8 1.6 %collective-permute-start.18 = (f32[64,128]{1,0:T(8,128)S(1)}, f32[64,128]{1,0:T(8,128)S(1)}, u32[]{:S(2)}, u32[]{:S(2)}) collective-permute-start(f32[64,128]{1,0:T(8,128)S(1)} %add.37.refs_4_), channel_id=1, source_target_pairs={{0,6},{1,7},{2,4},{3,5},{4,2},{5,3},{6,0},{7,1},{8,14},{9,15},{10,... | collective-permute-start | bytes 98312 | tf_op jit(solution)/shard_map/ppermute | solution.py:1444
  72.4 0.8 copy.42
  73.2 0.4 copy.50
  73.9 0.5 fusion
  74.4 2.0 %copy.39 = f32[1,1,2,1,18,18,320]{6,3,5,4,2,1,0:T(1,128)} copy(f32[1,1,2,1,18,18,320]{6,2,5,4,3,1,0:T(2,128)S(1)} %fusion) | data formatting | bytes 1658880 | tf_op jit(solution)/shard_map/reshape | solution.py:1549
  76.4 2.2 %collective-permute-done.16.refs_5_ = f32[64,128]{1,0:T(8,128)S(1)} collective-permute-done((f32[64,128]{1,0:T(8,128)S(1)}, f32[64,128]{1,0:T(8,128)S(1)}, u32[]{:S(2)}, u32[]{:S(2)}) %collective-permute-start.16) | collective-permute-done | bytes 32800 | tf_op jit(solution)/shard_map/ppermute | solution.py:1444
  78.6 0.8 collective-permute-done.17.refs_6_
  79.4 0.6 collective-permute-done.18.refs_7_
  80.2 3.6 %all-to-all-start = ((bf16[8,9,36,128]{3,2,1,0:T(8,128)(2,1)}), bf16[8,9,36,128]{3,2,1,0:T(8,128)(2,1)S(1)}, u32[]{:S(2)}, u32[]{:S(2)}) async-start(bf16[8,9,36,128]{3,2,1,0:T(8,128)(2,1)} %get-tuple-element.107), calls=%async_computation | async-start | bytes 1474560 | tf_op jit(solution)/shard_map/all_to_all | solution.py:1439
  83.7 1.6 %collective-permute-start.19 = (bf16[11,32,128]{2,1,0:T(8,128)(2,1)S(1)}, bf16[11,32,128]{2,1,0:T(8,128)(2,1)S(1)}, u32[]{:S(2)}, u32[]{:S(2)}) collective-permute-start(bf16[11,32,128]{2,1,0:T(8,128)(2,1)S(1)} %get-tuple-element.109), channel_id=1, source_target_pairs={{0,8},{8,16},{16,24},{24,0},{1,9},{9,17},{17,25},{25,1},{2,10},{10... | collective-permute-start | bytes 270344 | tf_op jit(solution)/shard_map/ppermute | solution.py:1556
  85.4 2.5 %collective-permute-start.20 = (bf16[11,32,128]{2,1,0:T(8,128)(2,1)S(1)}, bf16[11,32,128]{2,1,0:T(8,128)(2,1)S(1)}, u32[]{:S(2)}, u32[]{:S(2)}) collective-permute-start(bf16[11,32,128]{2,1,0:T(8,128)(2,1)S(1)} %get-tuple-element.110), channel_id=1, source_target_pairs={{0,16},{8,24},{16,0},{24,8},{1,17},{9,25},{17,1},{25,9},{2,18},{10... | collective-permute-start | bytes 270344 | tf_op jit(solution)/shard_map/ppermute | solution.py:1556
  87.9 1.3 %collective-permute-start.21 = (bf16[11,32,128]{2,1,0:T(8,128)(2,1)S(1)}, bf16[11,32,128]{2,1,0:T(8,128)(2,1)S(1)}, u32[]{:S(2)}, u32[]{:S(2)}) collective-permute-start(bf16[11,32,128]{2,1,0:T(8,128)(2,1)S(1)} %get-tuple-element.111), channel_id=1, source_target_pairs={{0,24},{8,0},{16,8},{24,16},{1,25},{9,1},{17,9},{25,17},{2,26},{10... | collective-permute-start | bytes 270344 | tf_op jit(solution)/shard_map/ppermute | solution.py:1556
  89.2 1.9 %collective-permute-done.19.refs_1_ = bf16[11,32,128]{2,1,0:T(8,128)(2,1)S(1)} collective-permute-done((bf16[11,32,128]{2,1,0:T(8,128)(2,1)S(1)}, bf16[11,32,128]{2,1,0:T(8,128)(2,1)S(1)}, u32[]{:S(2)}, u32[]{:S(2)}) %collective-permute-start.19) | collective-permute-done | bytes 90144 | tf_op jit(solution)/shard_map/ppermute | solution.py:1556
  91.1 3.3 %collective-permute-done.20.refs_2_ = bf16[11,32,128]{2,1,0:T(8,128)(2,1)S(1)} collective-permute-done((bf16[11,32,128]{2,1,0:T(8,128)(2,1)S(1)}, bf16[11,32,128]{2,1,0:T(8,128)(2,1)S(1)}, u32[]{:S(2)}, u32[]{:S(2)}) %collective-permute-start.20) | collective-permute-done | bytes 90144 | tf_op jit(solution)/shard_map/ppermute | solution.py:1556
  94.4 0.8 fold_batch.1
  95.2 2.4 %collective-permute-start.22 = (bf16[11,32,128]{2,1,0:T(8,128)(2,1)S(1)}, bf16[11,32,128]{2,1,0:T(8,128)(2,1)S(1)}, u32[]{:S(2)}, u32[]{:S(2)}) collective-permute-start(bf16[11,32,128]{2,1,0:T(8,128)(2,1)S(1)} %get-tuple-element.117.refs_0_), channel_id=1, source_target_pairs={{0,8},{8,16},{16,24},{24,0},{1,9},{9,17},{17,25},{25,1},{2,10},{10... | collective-permute-start | bytes 270344 | tf_op jit(solution)/shard_map/ppermute | solution.py:1566
  97.6 1.6 %collective-permute-start.23 = (bf16[11,32,128]{2,1,0:T(8,128)(2,1)S(1)}, bf16[11,32,128]{2,1,0:T(8,128)(2,1)S(1)}, u32[]{:S(2)}, u32[]{:S(2)}) collective-permute-start(bf16[11,32,128]{2,1,0:T(8,128)(2,1)S(1)} %get-tuple-element.117.refs_0_), channel_id=1, source_target_pairs={{0,16},{8,24},{16,0},{24,8},{1,17},{9,25},{17,1},{25,9},{2,18},{10... | collective-permute-start | bytes 270344 | tf_op jit(solution)/shard_map/ppermute | solution.py:1566
  99.2 0.8 collective-permute-start.24
  100.0 4.4 %all-to-all-start.1 = ((f32[32,1,128]{2,1,0:T(1,128)}), f32[32,1,128]{2,1,0:T(1,128)S(1)}, u32[]{:S(2)}, u32[]{:S(2)}) async-start(f32[32,1,128]{2,1,0:T(1,128)} %get-tuple-element.114), calls=%async_computation.1 | async-start | bytes 32768 | tf_op jit(solution)/shard_map/all_to_all | solution.py:1439
  104.4 1.2 bitcast_convert_fusion
  105.6 5.9 %all-to-all-done.1.norm_ref = f32[32,1,128]{2,1,0:T(1,128)S(1)} async-done(((f32[32,1,128]{2,1,0:T(1,128)}), f32[32,1,128]{2,1,0:T(1,128)S(1)}, u32[]{:S(2)}, u32[]{:S(2)}) %all-to-all-start.1) | async-done | bytes 16416 | tf_op jit(solution)/shard_map/all_to_all | solution.py:1439
  111.5 5.1 %update.1 = (f32[41,64,64]{2,1,0:T(8,128)}, f32[41,64,64]{2,1,0:T(8,128)}, f32[41,64,64]{2,1,0:T(8,128)}, f32[41,64,64]{2,1,0:T(8,128)}, bf16[41,64,64]{2,1,0:T(...) custom-call(s32[1]{0:T(128)} %bitcast.14.spot_ref, f32[32,1,128]{2,1,0:T(1,128)S(1)} %all-to-all-done.1.norm_ref, ...), custom_call_target="tpu_custom_call" | custom-call | tf_op jit(solution)/shard_map/update/pallas_call | solution.py:1418
  116.7 0.7 divide_subtract_fusion
  (45 shorter events, 1.5 us)
Async XLA Ops:
  0.6 6.5 %copy-start.1 = (s32[16]{0:T(128)S(1)}, s32[16]{0:T(128)}, u32[]{:S(2)}) copy-start(s32[16]{0:T(128)} %bucket_ref.5) | copy-start | bytes 196
  0.7 6.7 %copy-start.3 = (bf16[1,1,2,1,18,18,320]{6,2,5,4,3,1,0:T(2,128)(2,1)S(1)}, bf16[1,1,2,1,18,18,320]{6,2,5,4,3,1,0:T(2,128)(2,1)}, u32[]{:S(2)}) copy-start(bf16[1,1,2,1,18,18,320]{6,2,5,4,3,1,0:T(2,128)(2,1)} %param.14) | copy-start | bytes 1244164
  2.6 7.4 %copy-start.5 = (s32[328]{0:T(512)S(1)}, s32[328]{0:T(512)}, u32[]{:S(2)}) copy-start(s32[328]{0:T(512)} %param.13) | copy-start | bytes 3940
  2.6 15.4 %collective-permute-start = (bf16[1984,128]{1,0:T(8,128)(2,1)S(1)}, bf16[1984,128]{1,0:T(8,128)(2,1)S(1)}, u32[]{:S(2)}, u32[]{:S(2)}) collective-permute-start(bf16[1984,128]{1,0:T(8,128)(2,1)S(1)} %get-tuple-element.73), channel_id=1, source_target_pairs={{0,2},{1,3},{2,0},{3,1},{4,6},{5,7},{6,4},{7,5},{8,10},{9,11},{10,... | collective-permute-start | bytes 1523720 | tf_op jit(solution)/shard_map/ppermute | solution.py:1444
  5.6 16.7 %collective-permute-start.1 = (bf16[1984,128]{1,0:T(8,128)(2,1)S(1)}, bf16[1984,128]{1,0:T(8,128)(2,1)S(1)}, u32[]{:S(2)}, u32[]{:S(2)}) collective-permute-start(bf16[1984,128]{1,0:T(8,128)(2,1)S(1)} %get-tuple-element.74), channel_id=1, source_target_pairs={{0,4},{1,5},{2,6},{3,7},{4,0},{5,1},{6,2},{7,3},{8,12},{9,13},{10,... | collective-permute-start | bytes 1523720 | tf_op jit(solution)/shard_map/ppermute | solution.py:1444
  8.6 22.1 %copy-start = (f32[5248]{0:T(1024)S(1)}, f32[5248]{0:T(1024)}, u32[]{:S(2)}) copy-start(f32[5248]{0:T(1024)} %param.20) | copy-start | bytes 62980
  10.2 12.1 %collective-permute-start.2 = (bf16[672,128]{1,0:T(8,128)(2,1)S(1)}, bf16[672,128]{1,0:T(8,128)(2,1)S(1)}, u32[]{:S(2)}, u32[]{:S(2)}) collective-permute-start(bf16[672,128]{1,0:T(8,128)(2,1)S(1)} %get-tuple-element.75), channel_id=1, source_target_pairs={{0,6},{1,7},{2,4},{3,5},{4,2},{5,3},{6,0},{7,1},{8,14},{9,15},{10,... | collective-permute-start | bytes 516104 | tf_op jit(solution)/shard_map/ppermute | solution.py:1444
  10.3 20.4 %collective-permute-start.3 = (bf16[1984,128]{1,0:T(8,128)(2,1)S(1)}, bf16[1984,128]{1,0:T(8,128)(2,1)S(1)}, u32[]{:S(2)}, u32[]{:S(2)}) collective-permute-start(bf16[1984,128]{1,0:T(8,128)(2,1)S(1)} %get-tuple-element.72.refs_0_), channel_id=1, source_target_pairs={{0,1},{1,0},{2,3},{3,2},{4,5},{5,4},{6,7},{7,6},{8,9},{9,8},{10,11... | collective-permute-start | bytes 1523720 | tf_op jit(solution)/shard_map/ppermute | solution.py:1444
  18.0 12.7 %collective-permute-start.4 = (bf16[1984,128]{1,0:T(8,128)(2,1)S(1)}, bf16[1984,128]{1,0:T(8,128)(2,1)S(1)}, u32[]{:S(2)}, u32[]{:S(2)}) collective-permute-start(bf16[1984,128]{1,0:T(8,128)(2,1)S(1)} %collective-permute-done.refs_1_), channel_id=1, source_target_pairs={{0,1},{1,0},{2,3},{3,2},{4,5},{5,4},{6,7},{7,6},{8,9},{9,8},{10,11... | collective-permute-start | bytes 1523720 | tf_op jit(solution)/shard_map/ppermute | solution.py:1444
  22.3 8.4 %collective-permute-start.5 = (bf16[1984,128]{1,0:T(8,128)(2,1)S(1)}, bf16[1984,128]{1,0:T(8,128)(2,1)S(1)}, u32[]{:S(2)}, u32[]{:S(2)}) collective-permute-start(bf16[1984,128]{1,0:T(8,128)(2,1)S(1)} %collective-permute-done.1.refs_2_), channel_id=1, source_target_pairs={{0,1},{1,0},{2,3},{3,2},{4,5},{5,4},{6,7},{7,6},{8,9},{9,8},{10,11... | collective-permute-start | bytes 1523720 | tf_op jit(solution)/shard_map/ppermute | solution.py:1444
  22.3 2.1 %collective-permute-start.6 = (bf16[672,128]{1,0:T(8,128)(2,1)S(1)}, bf16[672,128]{1,0:T(8,128)(2,1)S(1)}, u32[]{:S(2)}, u32[]{:S(2)}) collective-permute-start(bf16[672,128]{1,0:T(8,128)(2,1)S(1)} %collective-permute-done.2.refs_3_), channel_id=1, source_target_pairs={{0,1},{1,0},{2,3},{3,2},{4,5},{5,4},{6,7},{7,6},{8,9},{9,8},{10,11... | collective-permute-start | bytes 516104 | tf_op jit(solution)/shard_map/ppermute | solution.py:1444
  22.8 6.3 %collective-permute-start.7 = (bf16[672,128]{1,0:T(8,128)(2,1)S(1)}, bf16[672,128]{1,0:T(8,128)(2,1)S(1)}, u32[]{:S(2)}, u32[]{:S(2)}) collective-permute-start(bf16[672,128]{1,0:T(8,128)(2,1)S(1)} %slice.22), channel_id=1, source_target_pairs={{0,4},{1,5},{2,6},{3,7},{4,0},{5,1},{6,2},{7,3},{8,12},{9,13},{10,... | collective-permute-start | bytes 516104 | tf_op jit(solution)/shard_map/ppermute | solution.py:1444
  24.4 6.2 %collective-permute-start.8 = (bf16[640,128]{1,0:T(8,128)(2,1)S(1)}, bf16[640,128]{1,0:T(8,128)(2,1)S(1)}, u32[]{:S(2)}, u32[]{:S(2)}) collective-permute-start(bf16[640,128]{1,0:T(8,128)(2,1)S(1)} %slice.23), channel_id=1, source_target_pairs={{0,2},{1,3},{2,0},{3,1},{4,6},{5,7},{6,4},{7,5},{8,10},{9,11},{10,... | collective-permute-start | bytes 491528 | tf_op jit(solution)/shard_map/ppermute | solution.py:1444
  29.2 4.2 %collective-permute-start.9 = (bf16[672,128]{1,0:T(8,128)(2,1)S(1)}, bf16[672,128]{1,0:T(8,128)(2,1)S(1)}, u32[]{:S(2)}, u32[]{:S(2)}) collective-permute-start(bf16[672,128]{1,0:T(8,128)(2,1)S(1)} %collective-permute-done.7.refs_3_), channel_id=1, source_target_pairs={{0,1},{1,0},{2,3},{3,2},{4,5},{5,4},{6,7},{7,6},{8,9},{9,8},{10,11... | collective-permute-start | bytes 516104 | tf_op jit(solution)/shard_map/ppermute | solution.py:1444
  30.7 2.7 %collective-permute-start.10 = (bf16[640,128]{1,0:T(8,128)(2,1)S(1)}, bf16[640,128]{1,0:T(8,128)(2,1)S(1)}, u32[]{:S(2)}, u32[]{:S(2)}) collective-permute-start(bf16[640,128]{1,0:T(8,128)(2,1)S(1)} %collective-permute-done.8.refs_4_), channel_id=1, source_target_pairs={{0,1},{1,0},{2,3},{3,2},{4,5},{5,4},{6,7},{7,6},{8,9},{9,8},{10,11... | collective-permute-start | bytes 491528 | tf_op jit(solution)/shard_map/ppermute | solution.py:1444
  55.6 3.3 %collective-permute-start.11 = (bf16[165,32,128]{2,1,0:T(8,128)(2,1)S(1)}, bf16[165,32,128]{2,1,0:T(8,128)(2,1)S(1)}, u32[]{:S(2)}, u32[]{:S(2)}) collective-permute-start(bf16[165,32,128]{2,1,0:T(8,128)(2,1)S(1)} %get-tuple-element.88), channel_id=1, source_target_pairs={{0,1},{1,0},{2,3},{3,2},{4,5},{5,4},{6,7},{7,6},{8,9},{9,8},{10,11... | collective-permute-start | bytes 4055048 | tf_op jit(solution)/shard_map/ppermute | solution.py:1444
  59.9 10.9 %collective-permute-start.12 = (bf16[41,32,128]{2,1,0:T(8,128)(2,1)}, bf16[41,32,128]{2,1,0:T(8,128)(2,1)S(1)}, u32[]{:S(2)}, u32[]{:S(2)}) collective-permute-start(bf16[41,32,128]{2,1,0:T(8,128)(2,1)} %get-tuple-element.89), channel_id=1, source_target_pairs={{0,2},{1,3},{2,0},{3,1},{4,6},{5,7},{6,4},{7,5},{8,10},{9,11},{10,... | collective-permute-start | bytes 1007624 | tf_op jit(solution)/shard_map/ppermute | solution.py:1444
  60.4 19.6 %collective-permute-start.14 = (bf16[41,32,128]{2,1,0:T(8,128)(2,1)S(1)}, bf16[41,32,128]{2,1,0:T(8,128)(2,1)S(1)}, u32[]{:S(2)}, u32[]{:S(2)}) collective-permute-start(bf16[41,32,128]{2,1,0:T(8,128)(2,1)S(1)} %get-tuple-element.103), channel_id=1, source_target_pairs={{0,4},{1,5},{2,6},{3,7},{4,0},{5,1},{6,2},{7,3},{8,12},{9,13},{10,... | collective-permute-start | bytes 1007624 | tf_op jit(solution)/shard_map/ppermute | solution.py:1444
  62.0 17.9 %collective-permute-start.15 = (bf16[41,32,128]{2,1,0:T(8,128)(2,1)S(1)}, bf16[41,32,128]{2,1,0:T(8,128)(2,1)S(1)}, u32[]{:S(2)}, u32[]{:S(2)}) collective-permute-start(bf16[41,32,128]{2,1,0:T(8,128)(2,1)S(1)} %get-tuple-element.104), channel_id=1, source_target_pairs={{0,6},{1,7},{2,4},{3,5},{4,2},{5,3},{6,0},{7,1},{8,14},{9,15},{10,... | collective-permute-start | bytes 1007624 | tf_op jit(solution)/shard_map/ppermute | solution.py:1444
  67.2 1.3 %collective-permute-start.13 = (f32[64,128]{1,0:T(8,128)S(1)}, f32[64,128]{1,0:T(8,128)S(1)}, u32[]{:S(2)}, u32[]{:S(2)}) collective-permute-start(f32[64,128]{1,0:T(8,128)S(1)} %get-tuple-element.98), channel_id=1, source_target_pairs={{0,1},{1,0},{2,3},{3,2},{4,5},{5,4},{6,7},{7,6},{8,9},{9,8},{10,11... | collective-permute-start | bytes 98312 | tf_op jit(solution)/shard_map/ppermute | solution.py:1444
  68.5 10.0 %collective-permute-start.16 = (f32[64,128]{1,0:T(8,128)S(1)}, f32[64,128]{1,0:T(8,128)S(1)}, u32[]{:S(2)}, u32[]{:S(2)}) collective-permute-start(f32[64,128]{1,0:T(8,128)S(1)} %add.37.refs_4_), channel_id=1, source_target_pairs={{0,2},{1,3},{2,0},{3,1},{4,6},{5,7},{6,4},{7,5},{8,10},{9,11},{10,... | collective-permute-start | bytes 98312 | tf_op jit(solution)/shard_map/ppermute | solution.py:1444
  69.0 10.3 %collective-permute-start.17 = (f32[64,128]{1,0:T(8,128)S(1)}, f32[64,128]{1,0:T(8,128)S(1)}, u32[]{:S(2)}, u32[]{:S(2)}) collective-permute-start(f32[64,128]{1,0:T(8,128)S(1)} %add.37.refs_4_), channel_id=1, source_target_pairs={{0,4},{1,5},{2,6},{3,7},{4,0},{5,1},{6,2},{7,3},{8,12},{9,13},{10,... | collective-permute-start | bytes 98312 | tf_op jit(solution)/shard_map/ppermute | solution.py:1444
  70.8 9.1 %collective-permute-start.18 = (f32[64,128]{1,0:T(8,128)S(1)}, f32[64,128]{1,0:T(8,128)S(1)}, u32[]{:S(2)}, u32[]{:S(2)}) collective-permute-start(f32[64,128]{1,0:T(8,128)S(1)} %add.37.refs_4_), channel_id=1, source_target_pairs={{0,6},{1,7},{2,4},{3,5},{4,2},{5,3},{6,0},{7,1},{8,14},{9,15},{10,... | collective-permute-start | bytes 98312 | tf_op jit(solution)/shard_map/ppermute | solution.py:1444
  80.2 19.8 %all-to-all-start = ((bf16[8,9,36,128]{3,2,1,0:T(8,128)(2,1)}), bf16[8,9,36,128]{3,2,1,0:T(8,128)(2,1)S(1)}, u32[]{:S(2)}, u32[]{:S(2)}) async-start(bf16[8,9,36,128]{3,2,1,0:T(8,128)(2,1)} %get-tuple-element.107), calls=%async_computation | async-start | bytes 1474560 | tf_op jit(solution)/shard_map/all_to_all | solution.py:1439
  83.7 7.4 %collective-permute-start.19 = (bf16[11,32,128]{2,1,0:T(8,128)(2,1)S(1)}, bf16[11,32,128]{2,1,0:T(8,128)(2,1)S(1)}, u32[]{:S(2)}, u32[]{:S(2)}) collective-permute-start(bf16[11,32,128]{2,1,0:T(8,128)(2,1)S(1)} %get-tuple-element.109), channel_id=1, source_target_pairs={{0,8},{8,16},{16,24},{24,0},{1,9},{9,17},{17,25},{25,1},{2,10},{10... | collective-permute-start | bytes 270344 | tf_op jit(solution)/shard_map/ppermute | solution.py:1556
  85.4 9.1 %collective-permute-start.20 = (bf16[11,32,128]{2,1,0:T(8,128)(2,1)S(1)}, bf16[11,32,128]{2,1,0:T(8,128)(2,1)S(1)}, u32[]{:S(2)}, u32[]{:S(2)}) collective-permute-start(bf16[11,32,128]{2,1,0:T(8,128)(2,1)S(1)} %get-tuple-element.110), channel_id=1, source_target_pairs={{0,16},{8,24},{16,0},{24,8},{1,17},{9,25},{17,1},{25,9},{2,18},{10... | collective-permute-start | bytes 270344 | tf_op jit(solution)/shard_map/ppermute | solution.py:1556
  87.9 6.6 %collective-permute-start.21 = (bf16[11,32,128]{2,1,0:T(8,128)(2,1)S(1)}, bf16[11,32,128]{2,1,0:T(8,128)(2,1)S(1)}, u32[]{:S(2)}, u32[]{:S(2)}) collective-permute-start(bf16[11,32,128]{2,1,0:T(8,128)(2,1)S(1)} %get-tuple-element.111), channel_id=1, source_target_pairs={{0,24},{8,0},{16,8},{24,16},{1,25},{9,1},{17,9},{25,17},{2,26},{10... | collective-permute-start | bytes 270344 | tf_op jit(solution)/shard_map/ppermute | solution.py:1556
  95.2 16.3 %collective-permute-start.22 = (bf16[11,32,128]{2,1,0:T(8,128)(2,1)S(1)}, bf16[11,32,128]{2,1,0:T(8,128)(2,1)S(1)}, u32[]{:S(2)}, u32[]{:S(2)}) collective-permute-start(bf16[11,32,128]{2,1,0:T(8,128)(2,1)S(1)} %get-tuple-element.117.refs_0_), channel_id=1, source_target_pairs={{0,8},{8,16},{16,24},{24,0},{1,9},{9,17},{17,25},{25,1},{2,10},{10... | collective-permute-start | bytes 270344 | tf_op jit(solution)/shard_map/ppermute | solution.py:1566
  97.6 13.9 %collective-permute-start.23 = (bf16[11,32,128]{2,1,0:T(8,128)(2,1)S(1)}, bf16[11,32,128]{2,1,0:T(8,128)(2,1)S(1)}, u32[]{:S(2)}, u32[]{:S(2)}) collective-permute-start(bf16[11,32,128]{2,1,0:T(8,128)(2,1)S(1)} %get-tuple-element.117.refs_0_), channel_id=1, source_target_pairs={{0,16},{8,24},{16,0},{24,8},{1,17},{9,25},{17,1},{25,9},{2,18},{10... | collective-permute-start | bytes 270344 | tf_op jit(solution)/shard_map/ppermute | solution.py:1566
  99.2 12.3 %collective-permute-start.24 = (bf16[11,32,128]{2,1,0:T(8,128)(2,1)S(1)}, bf16[11,32,128]{2,1,0:T(8,128)(2,1)S(1)}, u32[]{:S(2)}, u32[]{:S(2)}) collective-permute-start(bf16[11,32,128]{2,1,0:T(8,128)(2,1)S(1)} %get-tuple-element.117.refs_0_), channel_id=1, source_target_pairs={{0,24},{8,0},{16,8},{24,16},{1,25},{9,1},{17,9},{25,17},{2,26},{10... | collective-permute-start | bytes 270344 | tf_op jit(solution)/shard_map/ppermute | solution.py:1566
  100.0 11.5 %all-to-all-start.1 = ((f32[32,1,128]{2,1,0:T(1,128)}), f32[32,1,128]{2,1,0:T(1,128)S(1)}, u32[]{:S(2)}, u32[]{:S(2)}) async-start(f32[32,1,128]{2,1,0:T(1,128)} %get-tuple-element.114), calls=%async_computation.1 | async-start | bytes 32768 | tf_op jit(solution)/shard_map/all_to_all | solution.py:1439
  105.6 11.1 %copy-start.4 = (f32[656]{0:T(1024)S(1)}, f32[656]{0:T(1024)}, u32[]{:S(2)}) copy-start(f32[656]{0:T(1024)} %param.21) | copy-start | bytes 7876
  116.6 0.7 copy-start.2
where the time goes:
time: 118 us; the launch traced here: 117 us
  Pallas kernels  37.7 us (32%)
  waiting for transfers between devices  36.3 us (31%)
  starting transfers between devices  33.5 us (28%)
  local copies, waits for them, and re-layouts  4.99 us (4%)
  other arithmetic  3.95 us (3%)
    ppermute x19, waiting for transfers between devices, swap(): lax.ppermute(piece, 'tile', [(i, i ^ distance) for i in range(count)])  25.2 us
    pallas_call x1, Pallas kernels, run_main(): pl.pallas_call(functools.partial(main_kernel, pairs, strip_count, slots),...  20.7 us
    ppermute x19, starting transfers between devices, swap(): lax.ppermute(piece, 'tile', [(i, i ^ distance) for i in range(count)])  15.3 us
    all_to_all x2, starting transfers between devices, share_out(): return lax.all_to_all(pieces, axis, split_axis=0, concat_axis=0, tiled=True)  7.98 us
    all_to_all x2, waiting for transfers between devices, share_out(): return lax.all_to_all(pieces, axis, split_axis=0, concat_axis=0, tiled=True)  5.91 us
    ppermute x3, starting transfers between devices, on_device(): lax.ppermute(part, 'batch', [(i, (i + k + 1) % batch_count) for i in rang...  5.48 us
    ppermute x3, waiting for transfers between devices, on_device(): lax.ppermute(part, 'batch', [(i, (i + k + 1) % batch_count) for i in rang...  5.24 us
    pallas_call x1, Pallas kernels, update(): pl.pallas_call(functools.partial(update_kernel, shape[0], groups), in_spe...  5.13 us
  transfers between devices with their start and end apart: 27, of which 13 were waited for; matrix products, arithmetic and copies ran while one was open for 7% of the time, Pallas kernels for 6%

commit v1 on v0

--- a/solution.py
+++ b/solution.py
@@ -27,6 +27,7 @@
 STEP = 2 * LINE
 STEPS = AREA // STEP
 HALF = BS // 2
+PART3 = HID3 // 2
 STRIP = SR * CW
 STRIP_ROWS = STRIP + -STRIP % 16
 
@@ -691,15 +692,15 @@
                 ref[place] += value
 
     def begin_chunk(at):
-        lanes = slice(at, at + 256)
+        lanes = slice(at, at + PART3)
         hid3_ref[:, lanes] = product(h3_ref[...], w3_ref[:, lanes])
         dhid3_ref[:, lanes] = product_nt(dy3_ref[...], w4_ref[lanes])
 
     begin_chunk(0)
-    for at in range(0, HID3, 256):
-        if at + 256 < HID3:
-            begin_chunk(at + 256)
-        for lane in (at, at + 128):
+    for at in range(0, HID3, PART3):
+        if at + PART3 < HID3:
+            begin_chunk(at + PART3)
+        for lane in range(at, at + PART3, 128):
             lanes = slice(lane, lane + 128)
             total = nothing
             for k in range(STEPS):
@@ -710,7 +711,7 @@
                 g3_ref[rows, lanes] = change.astype(bf16)
                 total = total + fold(change)
             acc_hid_three[:, lanes] += total
-        lanes = slice(at, at + 256)
+        lanes = slice(at, at + PART3)
         out = product(u3_ref[:, lanes], w4_ref[lanes])
         d_low = product_nt(g3_ref[:, lanes], w3_ref[:, lanes])
         result_ref[0] = out if at == 0 else result_ref[0] + out

time: 118 us -> 118 us (level)
  no operation moved by 1% of the time
where the time goes in v1:
time: 118 us
  Pallas kernels  38.3 us (32%)
  waiting for transfers between devices  36.4 us (31%)
  starting transfers between devices  33.5 us (28%)
  local copies, waits for them, and re-layouts  4.99 us (4%)
  other arithmetic  3.95 us (3%)
    ppermute x19, waiting for transfers between devices, swap(): lax.ppermute(piece, 'tile', [(i, i ^ distance) for i in range(count)])  25.2 us
    pallas_call x1, Pallas kernels, run_main(): pl.pallas_call(functools.partial(main_kernel, pairs, strip_count, slots),...  21.3 us
    ppermute x19, starting transfers between devices, swap(): lax.ppermute(piece, 'tile', [(i, i ^ distance) for i in range(count)])  15.1 us
    all_to_all x2, starting transfers between devices, share_out(): return lax.all_to_all(pieces, axis, split_axis=0, concat_axis=0, tiled=True)  8.02 us
    all_to_all x2, waiting for transfers between devices, share_out(): return lax.all_to_all(pieces, axis, split_axis=0, concat_axis=0, tiled=True)  5.91 us
    ppermute x3, starting transfers between devices, on_device(): lax.ppermute(part, 'batch', [(i, (i + k + 1) % batch_count) for i in rang...  5.56 us
    ppermute x3, waiting for transfers between devices, on_device(): lax.ppermute(part, 'batch', [(i, (i + k + 1) % batch_count) for i in rang...  5.25 us
    pallas_call x1, Pallas kernels, update(): pl.pallas_call(functools.partial(update_kernel, shape[0], groups), in_spe...  5.13 us
  transfers between devices with their start and end apart: 27, of which 13 were waited for; matrix products, arithmetic and copies ran while one was open for 7% of the time, Pallas kernels for 6%

profile of v1, /device:TPU:0, one launch (start us, length us, event | category | flops | bytes accessed | tf_op | source)
XLA Modules:
  0.0 118.0 jit_solution(14461724945780352963)
XLA Ops:
  0.7 1.9 %pack.1 = (bf16[1984,128]{1,0:T(8,128)(2,1)S(1)}, bf16[1984,128]{1,0:T(8,128)(2,1)S(1)}, bf16[1984,128]{1,0:T(8,128)(2,1)S(1)}, bf16[672,128]{1,0:T(8,128)(2,1)S(1)}) custom-call(s32[1]{0:T(128)} %bitcast.6.place_ref, f32[41,64,64]{2,1,0:T(8,128)} %refs_4_.1, bf16[9,36,8,128]{3,2,1,0:T(8,128)(2,1)} %bitcast.45), custom_call_target="tpu_custom_call" | custom-call | tf_op jit(solution)/shard_map/pack/pallas_call | solution.py:1192
  2.6 3.0 %collective-permute-start = (bf16[1984,128]{1,0:T(8,128)(2,1)S(1)}, bf16[1984,128]{1,0:T(8,128)(2,1)S(1)}, u32[]{:S(2)}, u32[]{:S(2)}) collective-permute-start(bf16[1984,128]{1,0:T(8,128)(2,1)S(1)} %get-tuple-element.73), channel_id=1, source_target_pairs={{0,2},{1,3},{2,0},{3,1},{4,6},{5,7},{6,4},{7,5},{8,10},{9,11},{10,... | collective-permute-start | bytes 1523720 | tf_op jit(solution)/shard_map/ppermute | solution.py:1445
  5.6 1.5 %collective-permute-start.1 = (bf16[1984,128]{1,0:T(8,128)(2,1)S(1)}, bf16[1984,128]{1,0:T(8,128)(2,1)S(1)}, u32[]{:S(2)}, u32[]{:S(2)}) collective-permute-start(bf16[1984,128]{1,0:T(8,128)(2,1)S(1)} %get-tuple-element.74), channel_id=1, source_target_pairs={{0,4},{1,5},{2,6},{3,7},{4,0},{5,1},{6,2},{7,3},{8,12},{9,13},{10,... | collective-permute-start | bytes 1523720 | tf_op jit(solution)/shard_map/ppermute | solution.py:1445
  7.4 1.2 %fusion.1 = bf16[1,14,18,2,320]{4,3,2,1,0:T(2,128)(2,1)} fusion(bf16[2,18,18,320]{3,0,2,1:T(2,128)(2,1)S(1)} %bitcast.43, pred[2]{0:T(512)(128)(4,1)S(1)} %compare_reduce_fusion, bf16[2,18,18,320]{3,0,1,2:T(2,128)(2,1)S(1)} %bitcast.44), kind=kLoop, calls=%fused_computation.7 | loop fusion | flops 161280 | bytes 1097216 | tf_op jit(solution)/shard_map/transpose | solution.py:1492
  8.6 1.3 %reshape.79 = bf16[1,14,36,320]{3,2,1,0:T(8,128)(2,1)S(1)} reshape(bf16[1,14,18,2,320]{4,3,2,1,0:T(2,128)(2,1)} %fusion.1) | data formatting | bytes 645120 | tf_op jit(solution)/shard_map/reshape | solution.py:1493
  10.3 7.6 %collective-permute-done.refs_1_ = bf16[1984,128]{1,0:T(8,128)(2,1)S(1)} collective-permute-done((bf16[1984,128]{1,0:T(8,128)(2,1)S(1)}, bf16[1984,128]{1,0:T(8,128)(2,1)S(1)}, u32[]{:S(2)}, u32[]{:S(2)}) %collective-permute-start) | collective-permute-done | bytes 507936 | tf_op jit(solution)/shard_map/ppermute | solution.py:1445
  18.0 4.3 %collective-permute-done.1.refs_2_ = bf16[1984,128]{1,0:T(8,128)(2,1)S(1)} collective-permute-done((bf16[1984,128]{1,0:T(8,128)(2,1)S(1)}, bf16[1984,128]{1,0:T(8,128)(2,1)S(1)}, u32[]{:S(2)}, u32[]{:S(2)}) %collective-permute-start.1) | collective-permute-done | bytes 507936 | tf_op jit(solution)/shard_map/ppermute | solution.py:1445
  22.3 0.5 collective-permute-start.6
  22.8 1.6 %collective-permute-start.7 = (bf16[672,128]{1,0:T(8,128)(2,1)S(1)}, bf16[672,128]{1,0:T(8,128)(2,1)S(1)}, u32[]{:S(2)}, u32[]{:S(2)}) collective-permute-start(bf16[672,128]{1,0:T(8,128)(2,1)S(1)} %slice.22), channel_id=1, source_target_pairs={{0,4},{1,5},{2,6},{3,7},{4,0},{5,1},{6,2},{7,3},{8,12},{9,13},{10,... | collective-permute-start | bytes 516104 | tf_op jit(solution)/shard_map/ppermute | solution.py:1445
  24.4 0.6 collective-permute-start.8
  25.0 4.1 %collective-permute-done.7.refs_3_ = bf16[672,128]{1,0:T(8,128)(2,1)S(1)} collective-permute-done((bf16[672,128]{1,0:T(8,128)(2,1)S(1)}, bf16[672,128]{1,0:T(8,128)(2,1)S(1)}, u32[]{:S(2)}, u32[]{:S(2)}) %collective-permute-start.7) | collective-permute-done | bytes 172064 | tf_op jit(solution)/shard_map/ppermute | solution.py:1445
  29.2 1.5 %collective-permute-done.8.refs_4_ = bf16[640,128]{1,0:T(8,128)(2,1)S(1)} collective-permute-done((bf16[640,128]{1,0:T(8,128)(2,1)S(1)}, bf16[640,128]{1,0:T(8,128)(2,1)S(1)}, u32[]{:S(2)}, u32[]{:S(2)}) %collective-permute-start.8) | collective-permute-done | bytes 163872 | tf_op jit(solution)/shard_map/ppermute | solution.py:1445
  30.7 2.7 %entry.1 = (f32[1,4,560,128]{3,2,1,0:T(8,128)S(1)}, f32[1,4,560,128]{3,2,1,0:T(8,128)S(1)}, f32[1,4,560,128]{3,2,1,0:T(8,128)S(1)}, f32[1,4,560,128]{3,2,1,0:T(8,128)S(1)}, f32[1,4,8,128]{3,2,1,0:T(8,128)S(1)}) custom-call(s32[1]{0:T(128)} %bitcast.6.place_ref, s32[16]{0:T(128)S(1)} %copy-done.1, f32[41,128]{1,0:T(8,128)S(1)} %bitcast.36, ...), custom_call_target="tpu_custom_call" | custom-call | tf_op jit(solution)/shard_map/entry/pallas_call | solution.py:386
  33.4 1.5 %unpack.1 = (bf16[128,512]{1,0:T(8,128)(2,1)S(1)}, bf16[512,128]{1,0:T(8,128)(2,1)S(1)}, bf16[1152,384]{1,0:T(8,128)(2,1)S(1)}, bf16[384,1280]{1,0:T(8,128)(2,1)S(1)}, bf16[1280,384]{1,0:T(8,128)(2,1)S(1)}) custom-call(s32[328]{0:T(512)S(1)} %get-tuple-element.80.slot_ref, bf16[1984,128]{1,0:T(8,128)(2,1)S(1)} %get-tuple-element.72.refs_0_, ...), custom_call_target="tpu_custom_call" | custom-call | tf_op jit(solution)/shard_map/unpack/pallas_call | solution.py:437
  34.9 21.3 %blocks.1 = (f32[1,560,384]{2,1,0:T(8,128)S(1)}, f32[1,4,560,128]{3,2,1,0:T(8,128)S(1)}, f32[1,4,560,128]{3,2,1,0:T(8,128)S(1)}, f32[1,2,8,128]{3,2,1,0:T(8,128)...) custom-call(s32[328]{0:T(512)S(1)} %compare_select_fusion.1.near_place, ...), custom_call_target="tpu_custom_call" | custom-call | tf_op jit(solution)/shard_map/blocks/pallas_call | solution.py:953
  56.2 0.6 collective-permute-start.11
  56.9 2.7 %collective-permute-done.11.got_ref = bf16[165,32,128]{2,1,0:T(8,128)(2,1)S(1)} collective-permute-done((bf16[165,32,128]{2,1,0:T(8,128)(2,1)S(1)}, bf16[165,32,128]{2,1,0:T(8,128)(2,1)S(1)}, u32[]{:S(2)}, u32[]{:S(2)}) %collective-permute-start.11) | collective-permute-done | bytes 1351712 | tf_op jit(solution)/shard_map/ppermute | solution.py:1445
  59.6 1.0 fold_pair.1
  60.6 0.4 collective-permute-start.12
  61.0 1.6 %collective-permute-start.14 = (bf16[41,32,128]{2,1,0:T(8,128)(2,1)S(1)}, bf16[41,32,128]{2,1,0:T(8,128)(2,1)S(1)}, u32[]{:S(2)}, u32[]{:S(2)}) collective-permute-start(bf16[41,32,128]{2,1,0:T(8,128)(2,1)S(1)} %get-tuple-element.103), channel_id=1, source_target_pairs={{0,4},{1,5},{2,6},{3,7},{4,0},{5,1},{6,2},{7,3},{8,12},{9,13},{10,... | collective-permute-start | bytes 1007624 | tf_op jit(solution)/shard_map/ppermute | solution.py:1445
  62.6 1.4 %collective-permute-start.15 = (bf16[41,32,128]{2,1,0:T(8,128)(2,1)S(1)}, bf16[41,32,128]{2,1,0:T(8,128)(2,1)S(1)}, u32[]{:S(2)}, u32[]{:S(2)}) collective-permute-start(bf16[41,32,128]{2,1,0:T(8,128)(2,1)S(1)} %get-tuple-element.104), channel_id=1, source_target_pairs={{0,6},{1,7},{2,4},{3,5},{4,2},{5,3},{6,0},{7,1},{8,14},{9,15},{10,... | collective-permute-start | bytes 1007624 | tf_op jit(solution)/shard_map/ppermute | solution.py:1445
  64.1 3.8 %exit.1 = (bf16[8,9,36,128]{3,2,1,0:T(8,128)(2,1)}, f32[64,128]{1,0:T(8,128)S(1)}) custom-call(s32[1]{0:T(128)} %bitcast.6.place_ref, s32[16]{0:T(128)S(1)} %copy-done.1, f32[1,4,560,128]{3,2,1,0:T(8,128)S(1)} %get-tuple-element.91.x_in, f32[1,4,560,128]{3,2,1,0:T(8,128)S(1)} %get-tuple-element.76.inv_in, f32[1,4,560,128]{3,2,1,0:T(8,128)S(1)} %get-tuple-element.92.pool_in, ...), custom_call_target="tpu_custom_call" | custom-call | tf_op jit(solution)/shard_map/exit/pallas_call | solution.py:1112
  68.0 1.2 %collective-permute-done.13 = f32[64,128]{1,0:T(8,128)S(1)} collective-permute-done((f32[64,128]{1,0:T(8,128)S(1)}, f32[64,128]{1,0:T(8,128)S(1)}, u32[]{:S(2)}, u32[]{:S(2)}) %collective-permute-start.13) | collective-permute-done | bytes 32800 | tf_op jit(solution)/shard_map/ppermute | solution.py:1445
  69.2 0.5 collective-permute-start.16
  69.7 1.6 %collective-permute-start.17 = (f32[64,128]{1,0:T(8,128)S(1)}, f32[64,128]{1,0:T(8,128)S(1)}, u32[]{:S(2)}, u32[]{:S(2)}) collective-permute-start(f32[64,128]{1,0:T(8,128)S(1)} %add.37.refs_4_), channel_id=1, source_target_pairs={{0,4},{1,5},{2,6},{3,7},{4,0},{5,1},{6,2},{7,3},{8,12},{9,13},{10,... | collective-permute-start | bytes 98312 | tf_op jit(solution)/shard_map/ppermute | solution.py:1445
  71.5 1.5 %collective-permute-start.18 = (f32[64,128]{1,0:T(8,128)S(1)}, f32[64,128]{1,0:T(8,128)S(1)}, u32[]{:S(2)}, u32[]{:S(2)}) collective-permute-start(f32[64,128]{1,0:T(8,128)S(1)} %add.37.refs_4_), channel_id=1, source_target_pairs={{0,6},{1,7},{2,4},{3,5},{4,2},{5,3},{6,0},{7,1},{8,14},{9,15},{10,... | collective-permute-start | bytes 98312 | tf_op jit(solution)/shard_map/ppermute | solution.py:1445
  73.0 0.8 copy.42
  73.8 0.4 copy.50
  74.5 0.5 fusion
  75.0 2.0 %copy.39 = f32[1,1,2,1,18,18,320]{6,3,5,4,2,1,0:T(1,128)} copy(f32[1,1,2,1,18,18,320]{6,2,5,4,3,1,0:T(2,128)S(1)} %fusion) | data formatting | bytes 1658880 | tf_op jit(solution)/shard_map/reshape | solution.py:1550
  77.0 2.3 %collective-permute-done.16.refs_5_ = f32[64,128]{1,0:T(8,128)S(1)} collective-permute-done((f32[64,128]{1,0:T(8,128)S(1)}, f32[64,128]{1,0:T(8,128)S(1)}, u32[]{:S(2)}, u32[]{:S(2)}) %collective-permute-start.16) | collective-permute-done | bytes 32800 | tf_op jit(solution)/shard_map/ppermute | solution.py:1445
  79.3 0.7 collective-permute-done.17.refs_6_
  80.0 0.5 collective-permute-done.18.refs_7_
  80.7 3.6 %all-to-all-start = ((bf16[8,9,36,128]{3,2,1,0:T(8,128)(2,1)}), bf16[8,9,36,128]{3,2,1,0:T(8,128)(2,1)S(1)}, u32[]{:S(2)}, u32[]{:S(2)}) async-start(bf16[8,9,36,128]{3,2,1,0:T(8,128)(2,1)} %get-tuple-element.107), calls=%async_computation | async-start | bytes 1474560 | tf_op jit(solution)/shard_map/all_to_all | solution.py:1440
  84.2 1.7 %collective-permute-start.19 = (bf16[11,32,128]{2,1,0:T(8,128)(2,1)S(1)}, bf16[11,32,128]{2,1,0:T(8,128)(2,1)S(1)}, u32[]{:S(2)}, u32[]{:S(2)}) collective-permute-start(bf16[11,32,128]{2,1,0:T(8,128)(2,1)S(1)} %get-tuple-element.109), channel_id=1, source_target_pairs={{0,8},{8,16},{16,24},{24,0},{1,9},{9,17},{17,25},{25,1},{2,10},{10... | collective-permute-start | bytes 270344 | tf_op jit(solution)/shard_map/ppermute | solution.py:1557
  85.9 2.6 %collective-permute-start.20 = (bf16[11,32,128]{2,1,0:T(8,128)(2,1)S(1)}, bf16[11,32,128]{2,1,0:T(8,128)(2,1)S(1)}, u32[]{:S(2)}, u32[]{:S(2)}) collective-permute-start(bf16[11,32,128]{2,1,0:T(8,128)(2,1)S(1)} %get-tuple-element.110), channel_id=1, source_target_pairs={{0,16},{8,24},{16,0},{24,8},{1,17},{9,25},{17,1},{25,9},{2,18},{10... | collective-permute-start | bytes 270344 | tf_op jit(solution)/shard_map/ppermute | solution.py:1557
  88.5 1.3 %collective-permute-start.21 = (bf16[11,32,128]{2,1,0:T(8,128)(2,1)S(1)}, bf16[11,32,128]{2,1,0:T(8,128)(2,1)S(1)}, u32[]{:S(2)}, u32[]{:S(2)}) collective-permute-start(bf16[11,32,128]{2,1,0:T(8,128)(2,1)S(1)} %get-tuple-element.111), channel_id=1, source_target_pairs={{0,24},{8,0},{16,8},{24,16},{1,25},{9,1},{17,9},{25,17},{2,26},{10... | collective-permute-start | bytes 270344 | tf_op jit(solution)/shard_map/ppermute | solution.py:1557
  89.8 1.8 %collective-permute-done.19.refs_1_ = bf16[11,32,128]{2,1,0:T(8,128)(2,1)S(1)} collective-permute-done((bf16[11,32,128]{2,1,0:T(8,128)(2,1)S(1)}, bf16[11,32,128]{2,1,0:T(8,128)(2,1)S(1)}, u32[]{:S(2)}, u32[]{:S(2)}) %collective-permute-start.19) | collective-permute-done | bytes 90144 | tf_op jit(solution)/shard_map/ppermute | solution.py:1557
  91.6 3.4 %collective-permute-done.20.refs_2_ = bf16[11,32,128]{2,1,0:T(8,128)(2,1)S(1)} collective-permute-done((bf16[11,32,128]{2,1,0:T(8,128)(2,1)S(1)}, bf16[11,32,128]{2,1,0:T(8,128)(2,1)S(1)}, u32[]{:S(2)}, u32[]{:S(2)}) %collective-permute-start.20) | collective-permute-done | bytes 90144 | tf_op jit(solution)/shard_map/ppermute | solution.py:1557
  95.1 0.8 fold_batch.1
  95.8 2.4 %collective-permute-start.22 = (bf16[11,32,128]{2,1,0:T(8,128)(2,1)S(1)}, bf16[11,32,128]{2,1,0:T(8,128)(2,1)S(1)}, u32[]{:S(2)}, u32[]{:S(2)}) collective-permute-start(bf16[11,32,128]{2,1,0:T(8,128)(2,1)S(1)} %get-tuple-element.117.refs_0_), channel_id=1, source_target_pairs={{0,8},{8,16},{16,24},{24,0},{1,9},{9,17},{17,25},{25,1},{2,10},{10... | collective-permute-start | bytes 270344 | tf_op jit(solution)/shard_map/ppermute | solution.py:1567
  98.2 1.5 %collective-permute-start.23 = (bf16[11,32,128]{2,1,0:T(8,128)(2,1)S(1)}, bf16[11,32,128]{2,1,0:T(8,128)(2,1)S(1)}, u32[]{:S(2)}, u32[]{:S(2)}) collective-permute-start(bf16[11,32,128]{2,1,0:T(8,128)(2,1)S(1)} %get-tuple-element.117.refs_0_), channel_id=1, source_target_pairs={{0,16},{8,24},{16,0},{24,8},{1,17},{9,25},{17,1},{25,9},{2,18},{10... | collective-permute-start | bytes 270344 | tf_op jit(solution)/shard_map/ppermute | solution.py:1567
  99.8 0.8 collective-permute-start.24
  100.6 4.5 %all-to-all-start.1 = ((f32[32,1,128]{2,1,0:T(1,128)}), f32[32,1,128]{2,1,0:T(1,128)S(1)}, u32[]{:S(2)}, u32[]{:S(2)}) async-start(f32[32,1,128]{2,1,0:T(1,128)} %get-tuple-element.114), calls=%async_computation.1 | async-start | bytes 32768 | tf_op jit(solution)/shard_map/all_to_all | solution.py:1440
  105.1 1.2 bitcast_convert_fusion
  106.2 5.9 %all-to-all-done.1.norm_ref = f32[32,1,128]{2,1,0:T(1,128)S(1)} async-done(((f32[32,1,128]{2,1,0:T(1,128)}), f32[32,1,128]{2,1,0:T(1,128)S(1)}, u32[]{:S(2)}, u32[]{:S(2)}) %all-to-all-start.1) | async-done | bytes 16416 | tf_op jit(solution)/shard_map/all_to_all | solution.py:1440
  112.2 5.1 %update.1 = (f32[41,64,64]{2,1,0:T(8,128)}, f32[41,64,64]{2,1,0:T(8,128)}, f32[41,64,64]{2,1,0:T(8,128)}, f32[41,64,64]{2,1,0:T(8,128)}, bf16[41,64,64]{2,1,0:T(...) custom-call(s32[1]{0:T(128)} %bitcast.14.spot_ref, f32[32,1,128]{2,1,0:T(1,128)S(1)} %all-to-all-done.1.norm_ref, ...), custom_call_target="tpu_custom_call" | custom-call | tf_op jit(solution)/shard_map/update/pallas_call | solution.py:1419
  117.3 0.7 divide_subtract_fusion
  (45 shorter events, 1.6 us)
Async XLA Ops:
  0.6 6.5 %copy-start.1 = (s32[16]{0:T(128)S(1)}, s32[16]{0:T(128)}, u32[]{:S(2)}) copy-start(s32[16]{0:T(128)} %bucket_ref.5) | copy-start | bytes 196
  0.7 6.7 %copy-start.3 = (bf16[1,1,2,1,18,18,320]{6,2,5,4,3,1,0:T(2,128)(2,1)S(1)}, bf16[1,1,2,1,18,18,320]{6,2,5,4,3,1,0:T(2,128)(2,1)}, u32[]{:S(2)}) copy-start(bf16[1,1,2,1,18,18,320]{6,2,5,4,3,1,0:T(2,128)(2,1)} %param.14) | copy-start | bytes 1244164
  2.6 7.4 %copy-start.5 = (s32[328]{0:T(512)S(1)}, s32[328]{0:T(512)}, u32[]{:S(2)}) copy-start(s32[328]{0:T(512)} %param.13) | copy-start | bytes 3940
  2.6 15.4 %collective-permute-start = (bf16[1984,128]{1,0:T(8,128)(2,1)S(1)}, bf16[1984,128]{1,0:T(8,128)(2,1)S(1)}, u32[]{:S(2)}, u32[]{:S(2)}) collective-permute-start(bf16[1984,128]{1,0:T(8,128)(2,1)S(1)} %get-tuple-element.73), channel_id=1, source_target_pairs={{0,2},{1,3},{2,0},{3,1},{4,6},{5,7},{6,4},{7,5},{8,10},{9,11},{10,... | collective-permute-start | bytes 1523720 | tf_op jit(solution)/shard_map/ppermute | solution.py:1445
  5.6 16.7 %collective-permute-start.1 = (bf16[1984,128]{1,0:T(8,128)(2,1)S(1)}, bf16[1984,128]{1,0:T(8,128)(2,1)S(1)}, u32[]{:S(2)}, u32[]{:S(2)}) collective-permute-start(bf16[1984,128]{1,0:T(8,128)(2,1)S(1)} %get-tuple-element.74), channel_id=1, source_target_pairs={{0,4},{1,5},{2,6},{3,7},{4,0},{5,1},{6,2},{7,3},{8,12},{9,13},{10,... | collective-permute-start | bytes 1523720 | tf_op jit(solution)/shard_map/ppermute | solution.py:1445
  8.6 22.1 %copy-start = (f32[5248]{0:T(1024)S(1)}, f32[5248]{0:T(1024)}, u32[]{:S(2)}) copy-start(f32[5248]{0:T(1024)} %param.20) | copy-start | bytes 62980
  10.2 12.1 %collective-permute-start.2 = (bf16[672,128]{1,0:T(8,128)(2,1)S(1)}, bf16[672,128]{1,0:T(8,128)(2,1)S(1)}, u32[]{:S(2)}, u32[]{:S(2)}) collective-permute-start(bf16[672,128]{1,0:T(8,128)(2,1)S(1)} %get-tuple-element.75), channel_id=1, source_target_pairs={{0,6},{1,7},{2,4},{3,5},{4,2},{5,3},{6,0},{7,1},{8,14},{9,15},{10,... | collective-permute-start | bytes 516104 | tf_op jit(solution)/shard_map/ppermute | solution.py:1445
  10.3 20.4 %collective-permute-start.3 = (bf16[1984,128]{1,0:T(8,128)(2,1)S(1)}, bf16[1984,128]{1,0:T(8,128)(2,1)S(1)}, u32[]{:S(2)}, u32[]{:S(2)}) collective-permute-start(bf16[1984,128]{1,0:T(8,128)(2,1)S(1)} %get-tuple-element.72.refs_0_), channel_id=1, source_target_pairs={{0,1},{1,0},{2,3},{3,2},{4,5},{5,4},{6,7},{7,6},{8,9},{9,8},{10,11... | collective-permute-start | bytes 1523720 | tf_op jit(solution)/shard_map/ppermute | solution.py:1445
  18.0 12.7 %collective-permute-start.4 = (bf16[1984,128]{1,0:T(8,128)(2,1)S(1)}, bf16[1984,128]{1,0:T(8,128)(2,1)S(1)}, u32[]{:S(2)}, u32[]{:S(2)}) collective-permute-start(bf16[1984,128]{1,0:T(8,128)(2,1)S(1)} %collective-permute-done.refs_1_), channel_id=1, source_target_pairs={{0,1},{1,0},{2,3},{3,2},{4,5},{5,4},{6,7},{7,6},{8,9},{9,8},{10,11... | collective-permute-start | bytes 1523720 | tf_op jit(solution)/shard_map/ppermute | solution.py:1445
  22.3 8.4 %collective-permute-start.5 = (bf16[1984,128]{1,0:T(8,128)(2,1)S(1)}, bf16[1984,128]{1,0:T(8,128)(2,1)S(1)}, u32[]{:S(2)}, u32[]{:S(2)}) collective-permute-start(bf16[1984,128]{1,0:T(8,128)(2,1)S(1)} %collective-permute-done.1.refs_2_), channel_id=1, source_target_pairs={{0,1},{1,0},{2,3},{3,2},{4,5},{5,4},{6,7},{7,6},{8,9},{9,8},{10,11... | collective-permute-start | bytes 1523720 | tf_op jit(solution)/shard_map/ppermute | solution.py:1445
  22.3 2.1 %collective-permute-start.6 = (bf16[672,128]{1,0:T(8,128)(2,1)S(1)}, bf16[672,128]{1,0:T(8,128)(2,1)S(1)}, u32[]{:S(2)}, u32[]{:S(2)}) collective-permute-start(bf16[672,128]{1,0:T(8,128)(2,1)S(1)} %collective-permute-done.2.refs_3_), channel_id=1, source_target_pairs={{0,1},{1,0},{2,3},{3,2},{4,5},{5,4},{6,7},{7,6},{8,9},{9,8},{10,11... | collective-permute-start | bytes 516104 | tf_op jit(solution)/shard_map/ppermute | solution.py:1445
  22.8 6.3 %collective-permute-start.7 = (bf16[672,128]{1,0:T(8,128)(2,1)S(1)}, bf16[672,128]{1,0:T(8,128)(2,1)S(1)}, u32[]{:S(2)}, u32[]{:S(2)}) collective-permute-start(bf16[672,128]{1,0:T(8,128)(2,1)S(1)} %slice.22), channel_id=1, source_target_pairs={{0,4},{1,5},{2,6},{3,7},{4,0},{5,1},{6,2},{7,3},{8,12},{9,13},{10,... | collective-permute-start | bytes 516104 | tf_op jit(solution)/shard_map/ppermute | solution.py:1445
  24.4 6.2 %collective-permute-start.8 = (bf16[640,128]{1,0:T(8,128)(2,1)S(1)}, bf16[640,128]{1,0:T(8,128)(2,1)S(1)}, u32[]{:S(2)}, u32[]{:S(2)}) collective-permute-start(bf16[640,128]{1,0:T(8,128)(2,1)S(1)} %slice.23), channel_id=1, source_target_pairs={{0,2},{1,3},{2,0},{3,1},{4,6},{5,7},{6,4},{7,5},{8,10},{9,11},{10,... | collective-permute-start | bytes 491528 | tf_op jit(solution)/shard_map/ppermute | solution.py:1445
  29.2 4.2 %collective-permute-start.9 = (bf16[672,128]{1,0:T(8,128)(2,1)S(1)}, bf16[672,128]{1,0:T(8,128)(2,1)S(1)}, u32[]{:S(2)}, u32[]{:S(2)}) collective-permute-start(bf16[672,128]{1,0:T(8,128)(2,1)S(1)} %collective-permute-done.7.refs_3_), channel_id=1, source_target_pairs={{0,1},{1,0},{2,3},{3,2},{4,5},{5,4},{6,7},{7,6},{8,9},{9,8},{10,11... | collective-permute-start | bytes 516104 | tf_op jit(solution)/shard_map/ppermute | solution.py:1445
  30.7 2.7 %collective-permute-start.10 = (bf16[640,128]{1,0:T(8,128)(2,1)S(1)}, bf16[640,128]{1,0:T(8,128)(2,1)S(1)}, u32[]{:S(2)}, u32[]{:S(2)}) collective-permute-start(bf16[640,128]{1,0:T(8,128)(2,1)S(1)} %collective-permute-done.8.refs_4_), channel_id=1, source_target_pairs={{0,1},{1,0},{2,3},{3,2},{4,5},{5,4},{6,7},{7,6},{8,9},{9,8},{10,11... | collective-permute-start | bytes 491528 | tf_op jit(solution)/shard_map/ppermute | solution.py:1445
  56.2 3.4 %collective-permute-start.11 = (bf16[165,32,128]{2,1,0:T(8,128)(2,1)S(1)}, bf16[165,32,128]{2,1,0:T(8,128)(2,1)S(1)}, u32[]{:S(2)}, u32[]{:S(2)}) collective-permute-start(bf16[165,32,128]{2,1,0:T(8,128)(2,1)S(1)} %get-tuple-element.88), channel_id=1, source_target_pairs={{0,1},{1,0},{2,3},{3,2},{4,5},{5,4},{6,7},{7,6},{8,9},{9,8},{10,11... | collective-permute-start | bytes 4055048 | tf_op jit(solution)/shard_map/ppermute | solution.py:1445
  60.6 10.9 %collective-permute-start.12 = (bf16[41,32,128]{2,1,0:T(8,128)(2,1)}, bf16[41,32,128]{2,1,0:T(8,128)(2,1)S(1)}, u32[]{:S(2)}, u32[]{:S(2)}) collective-permute-start(bf16[41,32,128]{2,1,0:T(8,128)(2,1)} %get-tuple-element.89), channel_id=1, source_target_pairs={{0,2},{1,3},{2,0},{3,1},{4,6},{5,7},{6,4},{7,5},{8,10},{9,11},{10,... | collective-permute-start | bytes 1007624 | tf_op jit(solution)/shard_map/ppermute | solution.py:1445
  61.0 19.5 %collective-permute-start.14 = (bf16[41,32,128]{2,1,0:T(8,128)(2,1)S(1)}, bf16[41,32,128]{2,1,0:T(8,128)(2,1)S(1)}, u32[]{:S(2)}, u32[]{:S(2)}) collective-permute-start(bf16[41,32,128]{2,1,0:T(8,128)(2,1)S(1)} %get-tuple-element.103), channel_id=1, source_target_pairs={{0,4},{1,5},{2,6},{3,7},{4,0},{5,1},{6,2},{7,3},{8,12},{9,13},{10,... | collective-permute-start | bytes 1007624 | tf_op jit(solution)/shard_map/ppermute | solution.py:1445
  62.6 17.8 %collective-permute-start.15 = (bf16[41,32,128]{2,1,0:T(8,128)(2,1)S(1)}, bf16[41,32,128]{2,1,0:T(8,128)(2,1)S(1)}, u32[]{:S(2)}, u32[]{:S(2)}) collective-permute-start(bf16[41,32,128]{2,1,0:T(8,128)(2,1)S(1)} %get-tuple-element.104), channel_id=1, source_target_pairs={{0,6},{1,7},{2,4},{3,5},{4,2},{5,3},{6,0},{7,1},{8,14},{9,15},{10,... | collective-permute-start | bytes 1007624 | tf_op jit(solution)/shard_map/ppermute | solution.py:1445
  67.9 1.3 %collective-permute-start.13 = (f32[64,128]{1,0:T(8,128)S(1)}, f32[64,128]{1,0:T(8,128)S(1)}, u32[]{:S(2)}, u32[]{:S(2)}) collective-permute-start(f32[64,128]{1,0:T(8,128)S(1)} %get-tuple-element.98), channel_id=1, source_target_pairs={{0,1},{1,0},{2,3},{3,2},{4,5},{5,4},{6,7},{7,6},{8,9},{9,8},{10,11... | collective-permute-start | bytes 98312 | tf_op jit(solution)/shard_map/ppermute | solution.py:1445
  69.2 10.0 %collective-permute-start.16 = (f32[64,128]{1,0:T(8,128)S(1)}, f32[64,128]{1,0:T(8,128)S(1)}, u32[]{:S(2)}, u32[]{:S(2)}) collective-permute-start(f32[64,128]{1,0:T(8,128)S(1)} %add.37.refs_4_), channel_id=1, source_target_pairs={{0,2},{1,3},{2,0},{3,1},{4,6},{5,7},{6,4},{7,5},{8,10},{9,11},{10,... | collective-permute-start | bytes 98312 | tf_op jit(solution)/shard_map/ppermute | solution.py:1445
  69.7 10.3 %collective-permute-start.17 = (f32[64,128]{1,0:T(8,128)S(1)}, f32[64,128]{1,0:T(8,128)S(1)}, u32[]{:S(2)}, u32[]{:S(2)}) collective-permute-start(f32[64,128]{1,0:T(8,128)S(1)} %add.37.refs_4_), channel_id=1, source_target_pairs={{0,4},{1,5},{2,6},{3,7},{4,0},{5,1},{6,2},{7,3},{8,12},{9,13},{10,... | collective-permute-start | bytes 98312 | tf_op jit(solution)/shard_map/ppermute | solution.py:1445
  71.5 9.0 %collective-permute-start.18 = (f32[64,128]{1,0:T(8,128)S(1)}, f32[64,128]{1,0:T(8,128)S(1)}, u32[]{:S(2)}, u32[]{:S(2)}) collective-permute-start(f32[64,128]{1,0:T(8,128)S(1)} %add.37.refs_4_), channel_id=1, source_target_pairs={{0,6},{1,7},{2,4},{3,5},{4,2},{5,3},{6,0},{7,1},{8,14},{9,15},{10,... | collective-permute-start | bytes 98312 | tf_op jit(solution)/shard_map/ppermute | solution.py:1445
  80.7 19.9 %all-to-all-start = ((bf16[8,9,36,128]{3,2,1,0:T(8,128)(2,1)}), bf16[8,9,36,128]{3,2,1,0:T(8,128)(2,1)S(1)}, u32[]{:S(2)}, u32[]{:S(2)}) async-start(bf16[8,9,36,128]{3,2,1,0:T(8,128)(2,1)} %get-tuple-element.107), calls=%async_computation | async-start | bytes 1474560 | tf_op jit(solution)/shard_map/all_to_all | solution.py:1440
  84.2 7.4 %collective-permute-start.19 = (bf16[11,32,128]{2,1,0:T(8,128)(2,1)S(1)}, bf16[11,32,128]{2,1,0:T(8,128)(2,1)S(1)}, u32[]{:S(2)}, u32[]{:S(2)}) collective-permute-start(bf16[11,32,128]{2,1,0:T(8,128)(2,1)S(1)} %get-tuple-element.109), channel_id=1, source_target_pairs={{0,8},{8,16},{16,24},{24,0},{1,9},{9,17},{17,25},{25,1},{2,10},{10... | collective-permute-start | bytes 270344 | tf_op jit(solution)/shard_map/ppermute | solution.py:1557
  85.9 9.1 %collective-permute-start.20 = (bf16[11,32,128]{2,1,0:T(8,128)(2,1)S(1)}, bf16[11,32,128]{2,1,0:T(8,128)(2,1)S(1)}, u32[]{:S(2)}, u32[]{:S(2)}) collective-permute-start(bf16[11,32,128]{2,1,0:T(8,128)(2,1)S(1)} %get-tuple-element.110), channel_id=1, source_target_pairs={{0,16},{8,24},{16,0},{24,8},{1,17},{9,25},{17,1},{25,9},{2,18},{10... | collective-permute-start | bytes 270344 | tf_op jit(solution)/shard_map/ppermute | solution.py:1557
  88.5 6.5 %collective-permute-start.21 = (bf16[11,32,128]{2,1,0:T(8,128)(2,1)S(1)}, bf16[11,32,128]{2,1,0:T(8,128)(2,1)S(1)}, u32[]{:S(2)}, u32[]{:S(2)}) collective-permute-start(bf16[11,32,128]{2,1,0:T(8,128)(2,1)S(1)} %get-tuple-element.111), channel_id=1, source_target_pairs={{0,24},{8,0},{16,8},{24,16},{1,25},{9,1},{17,9},{25,17},{2,26},{10... | collective-permute-start | bytes 270344 | tf_op jit(solution)/shard_map/ppermute | solution.py:1557
  95.8 16.3 %collective-permute-start.22 = (bf16[11,32,128]{2,1,0:T(8,128)(2,1)S(1)}, bf16[11,32,128]{2,1,0:T(8,128)(2,1)S(1)}, u32[]{:S(2)}, u32[]{:S(2)}) collective-permute-start(bf16[11,32,128]{2,1,0:T(8,128)(2,1)S(1)} %get-tuple-element.117.refs_0_), channel_id=1, source_target_pairs={{0,8},{8,16},{16,24},{24,0},{1,9},{9,17},{17,25},{25,1},{2,10},{10... | collective-permute-start | bytes 270344 | tf_op jit(solution)/shard_map/ppermute | solution.py:1567
  98.2 13.9 %collective-permute-start.23 = (bf16[11,32,128]{2,1,0:T(8,128)(2,1)S(1)}, bf16[11,32,128]{2,1,0:T(8,128)(2,1)S(1)}, u32[]{:S(2)}, u32[]{:S(2)}) collective-permute-start(bf16[11,32,128]{2,1,0:T(8,128)(2,1)S(1)} %get-tuple-element.117.refs_0_), channel_id=1, source_target_pairs={{0,16},{8,24},{16,0},{24,8},{1,17},{9,25},{17,1},{25,9},{2,18},{10... | collective-permute-start | bytes 270344 | tf_op jit(solution)/shard_map/ppermute | solution.py:1567
  99.8 12.4 %collective-permute-start.24 = (bf16[11,32,128]{2,1,0:T(8,128)(2,1)S(1)}, bf16[11,32,128]{2,1,0:T(8,128)(2,1)S(1)}, u32[]{:S(2)}, u32[]{:S(2)}) collective-permute-start(bf16[11,32,128]{2,1,0:T(8,128)(2,1)S(1)} %get-tuple-element.117.refs_0_), channel_id=1, source_target_pairs={{0,24},{8,0},{16,8},{24,16},{1,25},{9,1},{17,9},{25,17},{2,26},{10... | collective-permute-start | bytes 270344 | tf_op jit(solution)/shard_map/ppermute | solution.py:1567
  100.6 11.5 %all-to-all-start.1 = ((f32[32,1,128]{2,1,0:T(1,128)}), f32[32,1,128]{2,1,0:T(1,128)S(1)}, u32[]{:S(2)}, u32[]{:S(2)}) async-start(f32[32,1,128]{2,1,0:T(1,128)} %get-tuple-element.114), calls=%async_computation.1 | async-start | bytes 32768 | tf_op jit(solution)/shard_map/all_to_all | solution.py:1440
  106.2 11.1 %copy-start.4 = (f32[656]{0:T(1024)S(1)}, f32[656]{0:T(1024)}, u32[]{:S(2)}) copy-start(f32[656]{0:T(1024)} %param.21) | copy-start | bytes 7876
  117.3 0.7 copy-start.2

commit v2 on v0

--- a/solution.py
+++ b/solution.py
@@ -1497,9 +1497,7 @@
         own, for_x, for_y, for_both = pack_pieces(
             place, master, pixels[0, 0].transpose(1, 2, 0, 3)
         )
-        goal, vec, slot_of, near_place, far_place, for_both = lax.optimization_barrier(
-            (goal, vec, slot_of, near_place, far_place, for_both)
-        )
+        goal, for_both = lax.optimization_barrier((goal, for_both))
         from_x, from_y, strips_both = swap(for_x, 2), swap(for_y, 4), swap(for_both, 6)
         near_half = (owned + 1) // 2
         middle = STRIP_ROWS + near_half * HALF

time: 118 us -> 117 us (level)
  waiting for transfers between devices: 36.3 us -> 34.7 us
  starting transfers between devices: 33.5 us -> 34.7 us
    ppermute x19, waiting for transfers between devices: 25.2 us -> 23.6 us  [swap(): lax.ppermute(piece, 'tile', [(i, i ^ distance) for i in range(count)])]
  transfers between devices with their start and end apart: 27 -> 27, of which waited for: 13 -> 10; matrix products, arithmetic and copies ran while one was open for 7% -> 7% of each run, Pallas kernels for 6% -> 6%
where the time goes in v2:
time: 117 us
  Pallas kernels  37.4 us (32%)
  starting transfers between devices  34.7 us (30%)
  waiting for transfers between devices  34.7 us (30%)
  local copies, waits for them, and re-layouts  4.99 us (4%)
  other arithmetic  3.95 us (3%)
    ppermute x19, waiting for transfers between devices, swap(): lax.ppermute(piece, 'tile', [(i, i ^ distance) for i in range(count)])  23.6 us
    pallas_call x1, Pallas kernels, run_main(): pl.pallas_call(functools.partial(main_kernel, pairs, strip_count, slots),...  20.6 us
    ppermute x19, starting transfers between devices, swap(): lax.ppermute(piece, 'tile', [(i, i ^ distance) for i in range(count)])  16.3 us
    all_to_all x2, starting transfers between devices, share_out(): return lax.all_to_all(pieces, axis, split_axis=0, concat_axis=0, tiled=True)  8.02 us
    all_to_all x2, waiting for transfers between devices, share_out(): return lax.all_to_all(pieces, axis, split_axis=0, concat_axis=0, tiled=True)  5.91 us
    ppermute x3, starting transfers between devices, on_device(): lax.ppermute(part, 'batch', [(i, (i + k + 1) % batch_count) for i in rang...  5.62 us
    ppermute x3, waiting for transfers between devices, on_device(): lax.ppermute(part, 'batch', [(i, (i + k + 1) % batch_count) for i in rang...  5.19 us
    pallas_call x1, Pallas kernels, update(): pl.pallas_call(functools.partial(update_kernel, shape[0], groups), in_spe...  5.13 us
  transfers between devices with their start and end apart: 27, of which 10 were waited for; matrix products, arithmetic and copies ran while one was open for 7% of the time, Pallas kernels for 6%

profile of v2, /device:TPU:0, one launch (start us, length us, event | category | flops | bytes accessed | tf_op | source)
XLA Modules:
  0.0 116.7 jit_solution(11924414813715022289)
XLA Ops:
  0.7 1.9 %pack.1 = (bf16[1984,128]{1,0:T(8,128)(2,1)S(1)}, bf16[1984,128]{1,0:T(8,128)(2,1)S(1)}, bf16[1984,128]{1,0:T(8,128)(2,1)S(1)}, bf16[672,128]{1,0:T(8,128)(2,1)S(1)}) custom-call(s32[1]{0:T(128)} %bitcast.place_ref, f32[41,64,64]{2,1,0:T(8,128)} %refs_4_.1, bf16[9,36,8,128]{3,2,1,0:T(8,128)(2,1)} %bitcast.45), custom_call_target="tpu_custom_call" | custom-call | tf_op jit(solution)/shard_map/pack/pallas_call | solution.py:1191
  2.6 3.0 %collective-permute-start = (bf16[1984,128]{1,0:T(8,128)(2,1)S(1)}, bf16[1984,128]{1,0:T(8,128)(2,1)S(1)}, u32[]{:S(2)}, u32[]{:S(2)}) collective-permute-start(bf16[1984,128]{1,0:T(8,128)(2,1)S(1)} %get-tuple-element.65), channel_id=1, source_target_pairs={{0,2},{1,3},{2,0},{3,1},{4,6},{5,7},{6,4},{7,5},{8,10},{9,11},{10,... | collective-permute-start | bytes 1523720 | tf_op jit(solution)/shard_map/ppermute | solution.py:1444
  5.6 1.5 %collective-permute-start.1 = (bf16[1984,128]{1,0:T(8,128)(2,1)S(1)}, bf16[1984,128]{1,0:T(8,128)(2,1)S(1)}, u32[]{:S(2)}, u32[]{:S(2)}) collective-permute-start(bf16[1984,128]{1,0:T(8,128)(2,1)S(1)} %get-tuple-element.66), channel_id=1, source_target_pairs={{0,4},{1,5},{2,6},{3,7},{4,0},{5,1},{6,2},{7,3},{8,12},{9,13},{10,... | collective-permute-start | bytes 1523720 | tf_op jit(solution)/shard_map/ppermute | solution.py:1444
  7.4 1.2 %fusion.1 = bf16[1,14,18,2,320]{4,3,2,1,0:T(2,128)(2,1)} fusion(bf16[2,18,18,320]{3,0,2,1:T(2,128)(2,1)S(1)} %bitcast.43, pred[2]{0:T(512)(128)(4,1)S(1)} %compare_reduce_fusion, bf16[2,18,18,320]{3,0,1,2:T(2,128)(2,1)S(1)} %bitcast.44), kind=kLoop, calls=%fused_computation.7 | loop fusion | flops 161280 | bytes 1097216 | tf_op jit(solution)/shard_map/transpose | solution.py:1491
  8.6 1.3 %reshape.81 = bf16[1,14,36,320]{3,2,1,0:T(8,128)(2,1)S(1)} reshape(bf16[1,14,18,2,320]{4,3,2,1,0:T(2,128)(2,1)} %fusion.1) | data formatting | bytes 645120 | tf_op jit(solution)/shard_map/reshape | solution.py:1492
  10.1 12.1 %collective-permute-done.2.refs_3_ = bf16[672,128]{1,0:T(8,128)(2,1)S(1)} collective-permute-done((bf16[672,128]{1,0:T(8,128)(2,1)S(1)}, bf16[672,128]{1,0:T(8,128)(2,1)S(1)}, u32[]{:S(2)}, u32[]{:S(2)}) %collective-permute-start.2) | collective-permute-done | bytes 172064 | tf_op jit(solution)/shard_map/ppermute | solution.py:1444
  22.1 0.5 collective-permute-start.3
  22.7 0.5 collective-permute-start.5
  23.3 0.7 collective-permute-start.7
  24.1 1.4 %collective-permute-start.8 = (bf16[640,128]{1,0:T(8,128)(2,1)S(1)}, bf16[640,128]{1,0:T(8,128)(2,1)S(1)}, u32[]{:S(2)}, u32[]{:S(2)}) collective-permute-start(bf16[640,128]{1,0:T(8,128)(2,1)S(1)} %slice.23), channel_id=1, source_target_pairs={{0,2},{1,3},{2,0},{3,1},{4,6},{5,7},{6,4},{7,5},{8,10},{9,11},{10,... | collective-permute-start | bytes 491528 | tf_op jit(solution)/shard_map/ppermute | solution.py:1444
  25.5 5.0 %collective-permute-done.8.refs_4_ = bf16[640,128]{1,0:T(8,128)(2,1)S(1)} collective-permute-done((bf16[640,128]{1,0:T(8,128)(2,1)S(1)}, bf16[640,128]{1,0:T(8,128)(2,1)S(1)}, u32[]{:S(2)}, u32[]{:S(2)}) %collective-permute-start.8) | collective-permute-done | bytes 163872 | tf_op jit(solution)/shard_map/ppermute | solution.py:1444
  30.5 0.5 collective-permute-start.9
  31.0 2.7 %entry.1 = (f32[1,4,560,128]{3,2,1,0:T(8,128)S(1)}, f32[1,4,560,128]{3,2,1,0:T(8,128)S(1)}, f32[1,4,560,128]{3,2,1,0:T(8,128)S(1)}, f32[1,4,560,128]{3,2,1,0:T(8,128)S(1)}, f32[1,4,8,128]{3,2,1,0:T(8,128)S(1)}) custom-call(s32[1]{0:T(128)} %bitcast.place_ref, s32[16]{0:T(128)S(1)} %copy-done.1, f32[41,128]{1,0:T(8,128)S(1)} %bitcast.36, ...), custom_call_target="tpu_custom_call" | custom-call | tf_op jit(solution)/shard_map/entry/pallas_call | solution.py:385
  33.7 1.5 %unpack.1 = (bf16[128,512]{1,0:T(8,128)(2,1)S(1)}, bf16[512,128]{1,0:T(8,128)(2,1)S(1)}, bf16[1152,384]{1,0:T(8,128)(2,1)S(1)}, bf16[384,1280]{1,0:T(8,128)(2,1)S(1)}, bf16[1280,384]{1,0:T(8,128)(2,1)S(1)}) custom-call(s32[328]{0:T(512)S(1)} %get-tuple-element.121.slot_ref, bf16[1984,128]{1,0:T(8,128)(2,1)S(1)} %get-tuple-element.64.refs_0_, ...), custom_call_target="tpu_custom_call" | custom-call | tf_op jit(solution)/shard_map/unpack/pallas_call | solution.py:436
  35.2 20.6 %blocks.1 = (f32[1,560,384]{2,1,0:T(8,128)S(1)}, f32[1,4,560,128]{3,2,1,0:T(8,128)S(1)}, f32[1,4,560,128]{3,2,1,0:T(8,128)S(1)}, f32[1,2,8,128]{3,2,1,0:T(8,128)...) custom-call(s32[328]{0:T(512)S(1)} %compare_select_fusion.1.near_place, ...), custom_call_target="tpu_custom_call" | custom-call | tf_op jit(solution)/shard_map/blocks/pallas_call | solution.py:952
  55.9 3.0 %collective-permute-done.11.got_ref = bf16[165,32,128]{2,1,0:T(8,128)(2,1)S(1)} collective-permute-done((bf16[165,32,128]{2,1,0:T(8,128)(2,1)S(1)}, bf16[165,32,128]{2,1,0:T(8,128)(2,1)S(1)}, u32[]{:S(2)}, u32[]{:S(2)}) %collective-permute-start.11) | collective-permute-done | bytes 1351712 | tf_op jit(solution)/shard_map/ppermute | solution.py:1444
  59.0 1.0 fold_pair.1
  60.0 0.8 collective-permute-start.12
  60.8 1.6 %collective-permute-start.14 = (bf16[41,32,128]{2,1,0:T(8,128)(2,1)S(1)}, bf16[41,32,128]{2,1,0:T(8,128)(2,1)S(1)}, u32[]{:S(2)}, u32[]{:S(2)}) collective-permute-start(bf16[41,32,128]{2,1,0:T(8,128)(2,1)S(1)} %get-tuple-element.95), channel_id=1, source_target_pairs={{0,4},{1,5},{2,6},{3,7},{4,0},{5,1},{6,2},{7,3},{8,12},{9,13},{10,... | collective-permute-start | bytes 1007624 | tf_op jit(solution)/shard_map/ppermute | solution.py:1444
  62.4 1.0 collective-permute-start.15
  63.5 3.7 %exit.1 = (bf16[8,9,36,128]{3,2,1,0:T(8,128)(2,1)}, f32[64,128]{1,0:T(8,128)S(1)}) custom-call(s32[1]{0:T(128)} %bitcast.place_ref, s32[16]{0:T(128)S(1)} %copy-done.1, f32[1,4,560,128]{3,2,1,0:T(8,128)S(1)} %get-tuple-element.83.x_in, f32[1,4,560,128]{3,2,1,0:T(8,128)S(1)} %get-tuple-element.69.inv_in, f32[1,4,560,128]{3,2,1,0:T(8,128)S(1)} %get-tuple-element.84.pool_in, ...), custom_call_target="tpu_custom_call" | custom-call | tf_op jit(solution)/shard_map/exit/pallas_call | solution.py:1111
  67.3 1.2 %collective-permute-done.13 = f32[64,128]{1,0:T(8,128)S(1)} collective-permute-done((f32[64,128]{1,0:T(8,128)S(1)}, f32[64,128]{1,0:T(8,128)S(1)}, u32[]{:S(2)}, u32[]{:S(2)}) %collective-permute-start.13) | collective-permute-done | bytes 32800 | tf_op jit(solution)/shard_map/ppermute | solution.py:1444
  68.5 0.8 collective-permute-start.16
  69.3 1.7 %collective-permute-start.17 = (f32[64,128]{1,0:T(8,128)S(1)}, f32[64,128]{1,0:T(8,128)S(1)}, u32[]{:S(2)}, u32[]{:S(2)}) collective-permute-start(f32[64,128]{1,0:T(8,128)S(1)} %add.37.refs_4_), channel_id=1, source_target_pairs={{0,4},{1,5},{2,6},{3,7},{4,0},{5,1},{6,2},{7,3},{8,12},{9,13},{10,... | collective-permute-start | bytes 98312 | tf_op jit(solution)/shard_map/ppermute | solution.py:1444
  71.0 1.8 %collective-permute-start.18 = (f32[64,128]{1,0:T(8,128)S(1)}, f32[64,128]{1,0:T(8,128)S(1)}, u32[]{:S(2)}, u32[]{:S(2)}) collective-permute-start(f32[64,128]{1,0:T(8,128)S(1)} %add.37.refs_4_), channel_id=1, source_target_pairs={{0,6},{1,7},{2,4},{3,5},{4,2},{5,3},{6,0},{7,1},{8,14},{9,15},{10,... | collective-permute-start | bytes 98312 | tf_op jit(solution)/shard_map/ppermute | solution.py:1444
  72.8 0.8 copy.42
  73.6 0.4 copy.50
  74.0 0.3 pad.9
  74.3 0.5 fusion
  74.8 2.0 %copy.39 = f32[1,1,2,1,18,18,320]{6,3,5,4,2,1,0:T(1,128)} copy(f32[1,1,2,1,18,18,320]{6,2,5,4,3,1,0:T(2,128)S(1)} %fusion) | data formatting | bytes 1658880 | tf_op jit(solution)/shard_map/reshape | solution.py:1547
  76.8 1.6 %collective-permute-done.16.refs_5_ = f32[64,128]{1,0:T(8,128)S(1)} collective-permute-done((f32[64,128]{1,0:T(8,128)S(1)}, f32[64,128]{1,0:T(8,128)S(1)}, u32[]{:S(2)}, u32[]{:S(2)}) %collective-permute-start.16) | collective-permute-done | bytes 32800 | tf_op jit(solution)/shard_map/ppermute | solution.py:1444
  78.4 0.4 collective-permute-done.17.refs_6_
  78.8 0.4 collective-permute-done.18.refs_7_
  79.3 3.6 %all-to-all-start = ((bf16[8,9,36,128]{3,2,1,0:T(8,128)(2,1)}), bf16[8,9,36,128]{3,2,1,0:T(8,128)(2,1)S(1)}, u32[]{:S(2)}, u32[]{:S(2)}) async-start(bf16[8,9,36,128]{3,2,1,0:T(8,128)(2,1)} %get-tuple-element.99), calls=%async_computation | async-start | bytes 1474560 | tf_op jit(solution)/shard_map/all_to_all | solution.py:1439
  82.9 1.7 %collective-permute-start.19 = (bf16[11,32,128]{2,1,0:T(8,128)(2,1)S(1)}, bf16[11,32,128]{2,1,0:T(8,128)(2,1)S(1)}, u32[]{:S(2)}, u32[]{:S(2)}) collective-permute-start(bf16[11,32,128]{2,1,0:T(8,128)(2,1)S(1)} %get-tuple-element.101), channel_id=1, source_target_pairs={{0,8},{8,16},{16,24},{24,0},{1,9},{9,17},{17,25},{25,1},{2,10},{10... | collective-permute-start | bytes 270344 | tf_op jit(solution)/shard_map/ppermute | solution.py:1554
  84.6 2.6 %collective-permute-start.20 = (bf16[11,32,128]{2,1,0:T(8,128)(2,1)S(1)}, bf16[11,32,128]{2,1,0:T(8,128)(2,1)S(1)}, u32[]{:S(2)}, u32[]{:S(2)}) collective-permute-start(bf16[11,32,128]{2,1,0:T(8,128)(2,1)S(1)} %get-tuple-element.102), channel_id=1, source_target_pairs={{0,16},{8,24},{16,0},{24,8},{1,17},{9,25},{17,1},{25,9},{2,18},{10... | collective-permute-start | bytes 270344 | tf_op jit(solution)/shard_map/ppermute | solution.py:1554
  87.2 1.3 %collective-permute-start.21 = (bf16[11,32,128]{2,1,0:T(8,128)(2,1)S(1)}, bf16[11,32,128]{2,1,0:T(8,128)(2,1)S(1)}, u32[]{:S(2)}, u32[]{:S(2)}) collective-permute-start(bf16[11,32,128]{2,1,0:T(8,128)(2,1)S(1)} %get-tuple-element.103), channel_id=1, source_target_pairs={{0,24},{8,0},{16,8},{24,16},{1,25},{9,1},{17,9},{25,17},{2,26},{10... | collective-permute-start | bytes 270344 | tf_op jit(solution)/shard_map/ppermute | solution.py:1554
  88.5 1.7 %collective-permute-done.19.refs_1_ = bf16[11,32,128]{2,1,0:T(8,128)(2,1)S(1)} collective-permute-done((bf16[11,32,128]{2,1,0:T(8,128)(2,1)S(1)}, bf16[11,32,128]{2,1,0:T(8,128)(2,1)S(1)}, u32[]{:S(2)}, u32[]{:S(2)}) %collective-permute-start.19) | collective-permute-done | bytes 90144 | tf_op jit(solution)/shard_map/ppermute | solution.py:1554
  90.3 3.4 %collective-permute-done.20.refs_2_ = bf16[11,32,128]{2,1,0:T(8,128)(2,1)S(1)} collective-permute-done((bf16[11,32,128]{2,1,0:T(8,128)(2,1)S(1)}, bf16[11,32,128]{2,1,0:T(8,128)(2,1)S(1)}, u32[]{:S(2)}, u32[]{:S(2)}) %collective-permute-start.20) | collective-permute-done | bytes 90144 | tf_op jit(solution)/shard_map/ppermute | solution.py:1554
  93.7 0.8 fold_batch.1
  94.5 2.4 %collective-permute-start.22 = (bf16[11,32,128]{2,1,0:T(8,128)(2,1)S(1)}, bf16[11,32,128]{2,1,0:T(8,128)(2,1)S(1)}, u32[]{:S(2)}, u32[]{:S(2)}) collective-permute-start(bf16[11,32,128]{2,1,0:T(8,128)(2,1)S(1)} %get-tuple-element.109.refs_0_), channel_id=1, source_target_pairs={{0,8},{8,16},{16,24},{24,0},{1,9},{9,17},{17,25},{25,1},{2,10},{10... | collective-permute-start | bytes 270344 | tf_op jit(solution)/shard_map/ppermute | solution.py:1564
  96.9 1.6 %collective-permute-start.23 = (bf16[11,32,128]{2,1,0:T(8,128)(2,1)S(1)}, bf16[11,32,128]{2,1,0:T(8,128)(2,1)S(1)}, u32[]{:S(2)}, u32[]{:S(2)}) collective-permute-start(bf16[11,32,128]{2,1,0:T(8,128)(2,1)S(1)} %get-tuple-element.109.refs_0_), channel_id=1, source_target_pairs={{0,16},{8,24},{16,0},{24,8},{1,17},{9,25},{17,1},{25,9},{2,18},{10... | collective-permute-start | bytes 270344 | tf_op jit(solution)/shard_map/ppermute | solution.py:1564
  98.5 0.8 collective-permute-start.24
  99.3 4.5 %all-to-all-start.1 = ((f32[32,1,128]{2,1,0:T(1,128)}), f32[32,1,128]{2,1,0:T(1,128)S(1)}, u32[]{:S(2)}, u32[]{:S(2)}) async-start(f32[32,1,128]{2,1,0:T(1,128)} %get-tuple-element.106), calls=%async_computation.1 | async-start | bytes 32768 | tf_op jit(solution)/shard_map/all_to_all | solution.py:1439
  103.7 1.2 %bitcast_convert_fusion = f32[1,1,8,9,36,128]{5,2,4,3,1,0:T(8,128)} fusion(bf16[8,9,36,128]{3,2,1,0:T(8,128)(2,1)S(1)} %all-to-all-done), kind=kLoop, calls=%fused_computation.4 | loop fusion | flops 331776 | bytes 1990656 | tf_op jit(solution)/shard_map/reshape | solution.py:1560
  104.9 5.9 %all-to-all-done.1.norm_ref = f32[32,1,128]{2,1,0:T(1,128)S(1)} async-done(((f32[32,1,128]{2,1,0:T(1,128)}), f32[32,1,128]{2,1,0:T(1,128)S(1)}, u32[]{:S(2)}, u32[]{:S(2)}) %all-to-all-start.1) | async-done | bytes 16416 | tf_op jit(solution)/shard_map/all_to_all | solution.py:1439
  110.8 5.1 %update.1 = (f32[41,64,64]{2,1,0:T(8,128)}, f32[41,64,64]{2,1,0:T(8,128)}, f32[41,64,64]{2,1,0:T(8,128)}, f32[41,64,64]{2,1,0:T(8,128)}, bf16[41,64,64]{2,1,0:T(...) custom-call(s32[1]{0:T(128)} %bitcast.14.spot_ref, f32[32,1,128]{2,1,0:T(1,128)S(1)} %all-to-all-done.1.norm_ref, ...), custom_call_target="tpu_custom_call" | custom-call | tf_op jit(solution)/shard_map/update/pallas_call | solution.py:1418
  116.0 0.7 divide_subtract_fusion
  (45 shorter events, 1.1 us)
Async XLA Ops:
  0.6 6.4 %copy-start.1 = (s32[16]{0:T(128)S(1)}, s32[16]{0:T(128)}, u32[]{:S(2)}) copy-start(s32[16]{0:T(128)} %bucket_ref.5) | copy-start | bytes 196
  0.7 6.7 %copy-start.3 = (bf16[1,1,2,1,18,18,320]{6,2,5,4,3,1,0:T(2,128)(2,1)S(1)}, bf16[1,1,2,1,18,18,320]{6,2,5,4,3,1,0:T(2,128)(2,1)}, u32[]{:S(2)}) copy-start(bf16[1,1,2,1,18,18,320]{6,2,5,4,3,1,0:T(2,128)(2,1)} %param.14) | copy-start | bytes 1244164
  2.6 20.1 %collective-permute-start = (bf16[1984,128]{1,0:T(8,128)(2,1)S(1)}, bf16[1984,128]{1,0:T(8,128)(2,1)S(1)}, u32[]{:S(2)}, u32[]{:S(2)}) collective-permute-start(bf16[1984,128]{1,0:T(8,128)(2,1)S(1)} %get-tuple-element.65), channel_id=1, source_target_pairs={{0,2},{1,3},{2,0},{3,1},{4,6},{5,7},{6,4},{7,5},{8,10},{9,11},{10,... | collective-permute-start | bytes 1523720 | tf_op jit(solution)/shard_map/ppermute | solution.py:1444
  5.6 17.1 %collective-permute-start.1 = (bf16[1984,128]{1,0:T(8,128)(2,1)S(1)}, bf16[1984,128]{1,0:T(8,128)(2,1)S(1)}, u32[]{:S(2)}, u32[]{:S(2)}) collective-permute-start(bf16[1984,128]{1,0:T(8,128)(2,1)S(1)} %get-tuple-element.66), channel_id=1, source_target_pairs={{0,4},{1,5},{2,6},{3,7},{4,0},{5,1},{6,2},{7,3},{8,12},{9,13},{10,... | collective-permute-start | bytes 1523720 | tf_op jit(solution)/shard_map/ppermute | solution.py:1444
  7.4 15.8 %copy-start.5 = (s32[328]{0:T(512)S(1)}, s32[328]{0:T(512)}, u32[]{:S(2)}) copy-start(s32[328]{0:T(512)} %param.13) | copy-start | bytes 3940
  8.6 22.4 %copy-start = (f32[5248]{0:T(1024)S(1)}, f32[5248]{0:T(1024)}, u32[]{:S(2)}) copy-start(f32[5248]{0:T(1024)} %param.20) | copy-start | bytes 62980
  10.0 12.1 %collective-permute-start.2 = (bf16[672,128]{1,0:T(8,128)(2,1)S(1)}, bf16[672,128]{1,0:T(8,128)(2,1)S(1)}, u32[]{:S(2)}, u32[]{:S(2)}) collective-permute-start(bf16[672,128]{1,0:T(8,128)(2,1)S(1)} %get-tuple-element.68), channel_id=1, source_target_pairs={{0,6},{1,7},{2,4},{3,5},{4,2},{5,3},{6,0},{7,1},{8,14},{9,15},{10,... | collective-permute-start | bytes 516104 | tf_op jit(solution)/shard_map/ppermute | solution.py:1444
  22.1 1.9 %collective-permute-start.6 = (bf16[672,128]{1,0:T(8,128)(2,1)S(1)}, bf16[672,128]{1,0:T(8,128)(2,1)S(1)}, u32[]{:S(2)}, u32[]{:S(2)}) collective-permute-start(bf16[672,128]{1,0:T(8,128)(2,1)S(1)} %collective-permute-done.2.refs_3_), channel_id=1, source_target_pairs={{0,1},{1,0},{2,3},{3,2},{4,5},{5,4},{6,7},{7,6},{8,9},{9,8},{10,11... | collective-permute-start | bytes 516104 | tf_op jit(solution)/shard_map/ppermute | solution.py:1444
  22.1 8.9 %collective-permute-start.3 = (bf16[1984,128]{1,0:T(8,128)(2,1)S(1)}, bf16[1984,128]{1,0:T(8,128)(2,1)S(1)}, u32[]{:S(2)}, u32[]{:S(2)}) collective-permute-start(bf16[1984,128]{1,0:T(8,128)(2,1)S(1)} %get-tuple-element.64.refs_0_), channel_id=1, source_target_pairs={{0,1},{1,0},{2,3},{3,2},{4,5},{5,4},{6,7},{7,6},{8,9},{9,8},{10,11... | collective-permute-start | bytes 1523720 | tf_op jit(solution)/shard_map/ppermute | solution.py:1444
  22.6 8.3 %collective-permute-start.4 = (bf16[1984,128]{1,0:T(8,128)(2,1)S(1)}, bf16[1984,128]{1,0:T(8,128)(2,1)S(1)}, u32[]{:S(2)}, u32[]{:S(2)}) collective-permute-start(bf16[1984,128]{1,0:T(8,128)(2,1)S(1)} %collective-permute-done.refs_1_), channel_id=1, source_target_pairs={{0,1},{1,0},{2,3},{3,2},{4,5},{5,4},{6,7},{7,6},{8,9},{9,8},{10,11... | collective-permute-start | bytes 1523720 | tf_op jit(solution)/shard_map/ppermute | solution.py:1444
  22.7 8.3 %collective-permute-start.5 = (bf16[1984,128]{1,0:T(8,128)(2,1)S(1)}, bf16[1984,128]{1,0:T(8,128)(2,1)S(1)}, u32[]{:S(2)}, u32[]{:S(2)}) collective-permute-start(bf16[1984,128]{1,0:T(8,128)(2,1)S(1)} %collective-permute-done.1.refs_2_), channel_id=1, source_target_pairs={{0,1},{1,0},{2,3},{3,2},{4,5},{5,4},{6,7},{7,6},{8,9},{9,8},{10,11... | collective-permute-start | bytes 1523720 | tf_op jit(solution)/shard_map/ppermute | solution.py:1444
  23.3 7.1 %collective-permute-start.7 = (bf16[672,128]{1,0:T(8,128)(2,1)S(1)}, bf16[672,128]{1,0:T(8,128)(2,1)S(1)}, u32[]{:S(2)}, u32[]{:S(2)}) collective-permute-start(bf16[672,128]{1,0:T(8,128)(2,1)S(1)} %slice.22), channel_id=1, source_target_pairs={{0,4},{1,5},{2,6},{3,7},{4,0},{5,1},{6,2},{7,3},{8,12},{9,13},{10,... | collective-permute-start | bytes 516104 | tf_op jit(solution)/shard_map/ppermute | solution.py:1444
  24.1 6.4 %collective-permute-start.8 = (bf16[640,128]{1,0:T(8,128)(2,1)S(1)}, bf16[640,128]{1,0:T(8,128)(2,1)S(1)}, u32[]{:S(2)}, u32[]{:S(2)}) collective-permute-start(bf16[640,128]{1,0:T(8,128)(2,1)S(1)} %slice.23), channel_id=1, source_target_pairs={{0,2},{1,3},{2,0},{3,1},{4,6},{5,7},{6,4},{7,5},{8,10},{9,11},{10,... | collective-permute-start | bytes 491528 | tf_op jit(solution)/shard_map/ppermute | solution.py:1444
  30.5 3.2 %collective-permute-start.10 = (bf16[640,128]{1,0:T(8,128)(2,1)S(1)}, bf16[640,128]{1,0:T(8,128)(2,1)S(1)}, u32[]{:S(2)}, u32[]{:S(2)}) collective-permute-start(bf16[640,128]{1,0:T(8,128)(2,1)S(1)} %collective-permute-done.8.refs_4_), channel_id=1, source_target_pairs={{0,1},{1,0},{2,3},{3,2},{4,5},{5,4},{6,7},{7,6},{8,9},{9,8},{10,11... | collective-permute-start | bytes 491528 | tf_op jit(solution)/shard_map/ppermute | solution.py:1444
  30.5 3.2 %collective-permute-start.9 = (bf16[672,128]{1,0:T(8,128)(2,1)S(1)}, bf16[672,128]{1,0:T(8,128)(2,1)S(1)}, u32[]{:S(2)}, u32[]{:S(2)}) collective-permute-start(bf16[672,128]{1,0:T(8,128)(2,1)S(1)} %collective-permute-done.7.refs_3_), channel_id=1, source_target_pairs={{0,1},{1,0},{2,3},{3,2},{4,5},{5,4},{6,7},{7,6},{8,9},{9,8},{10,11... | collective-permute-start | bytes 516104 | tf_op jit(solution)/shard_map/ppermute | solution.py:1444
  55.8 3.2 %collective-permute-start.11 = (bf16[165,32,128]{2,1,0:T(8,128)(2,1)S(1)}, bf16[165,32,128]{2,1,0:T(8,128)(2,1)S(1)}, u32[]{:S(2)}, u32[]{:S(2)}) collective-permute-start(bf16[165,32,128]{2,1,0:T(8,128)(2,1)S(1)} %get-tuple-element.80), channel_id=1, source_target_pairs={{0,1},{1,0},{2,3},{3,2},{4,5},{5,4},{6,7},{7,6},{8,9},{9,8},{10,11... | collective-permute-start | bytes 4055048 | tf_op jit(solution)/shard_map/ppermute | solution.py:1444
  60.0 11.0 %collective-permute-start.12 = (bf16[41,32,128]{2,1,0:T(8,128)(2,1)}, bf16[41,32,128]{2,1,0:T(8,128)(2,1)S(1)}, u32[]{:S(2)}, u32[]{:S(2)}) collective-permute-start(bf16[41,32,128]{2,1,0:T(8,128)(2,1)} %get-tuple-element.81), channel_id=1, source_target_pairs={{0,2},{1,3},{2,0},{3,1},{4,6},{5,7},{6,4},{7,5},{8,10},{9,11},{10,... | collective-permute-start | bytes 1007624 | tf_op jit(solution)/shard_map/ppermute | solution.py:1444
  60.8 18.3 %collective-permute-start.14 = (bf16[41,32,128]{2,1,0:T(8,128)(2,1)S(1)}, bf16[41,32,128]{2,1,0:T(8,128)(2,1)S(1)}, u32[]{:S(2)}, u32[]{:S(2)}) collective-permute-start(bf16[41,32,128]{2,1,0:T(8,128)(2,1)S(1)} %get-tuple-element.95), channel_id=1, source_target_pairs={{0,4},{1,5},{2,6},{3,7},{4,0},{5,1},{6,2},{7,3},{8,12},{9,13},{10,... | collective-permute-start | bytes 1007624 | tf_op jit(solution)/shard_map/ppermute | solution.py:1444
  62.4 16.7 %collective-permute-start.15 = (bf16[41,32,128]{2,1,0:T(8,128)(2,1)S(1)}, bf16[41,32,128]{2,1,0:T(8,128)(2,1)S(1)}, u32[]{:S(2)}, u32[]{:S(2)}) collective-permute-start(bf16[41,32,128]{2,1,0:T(8,128)(2,1)S(1)} %get-tuple-element.96), channel_id=1, source_target_pairs={{0,6},{1,7},{2,4},{3,5},{4,2},{5,3},{6,0},{7,1},{8,14},{9,15},{10,... | collective-permute-start | bytes 1007624 | tf_op jit(solution)/shard_map/ppermute | solution.py:1444
  67.2 1.3 %collective-permute-start.13 = (f32[64,128]{1,0:T(8,128)S(1)}, f32[64,128]{1,0:T(8,128)S(1)}, u32[]{:S(2)}, u32[]{:S(2)}) collective-permute-start(f32[64,128]{1,0:T(8,128)S(1)} %get-tuple-element.90), channel_id=1, source_target_pairs={{0,1},{1,0},{2,3},{3,2},{4,5},{5,4},{6,7},{7,6},{8,9},{9,8},{10,11... | collective-permute-start | bytes 98312 | tf_op jit(solution)/shard_map/ppermute | solution.py:1444
  68.5 9.9 %collective-permute-start.16 = (f32[64,128]{1,0:T(8,128)S(1)}, f32[64,128]{1,0:T(8,128)S(1)}, u32[]{:S(2)}, u32[]{:S(2)}) collective-permute-start(f32[64,128]{1,0:T(8,128)S(1)} %add.37.refs_4_), channel_id=1, source_target_pairs={{0,2},{1,3},{2,0},{3,1},{4,6},{5,7},{6,4},{7,5},{8,10},{9,11},{10,... | collective-permute-start | bytes 98312 | tf_op jit(solution)/shard_map/ppermute | solution.py:1444
  69.3 9.5 %collective-permute-start.17 = (f32[64,128]{1,0:T(8,128)S(1)}, f32[64,128]{1,0:T(8,128)S(1)}, u32[]{:S(2)}, u32[]{:S(2)}) collective-permute-start(f32[64,128]{1,0:T(8,128)S(1)} %add.37.refs_4_), channel_id=1, source_target_pairs={{0,4},{1,5},{2,6},{3,7},{4,0},{5,1},{6,2},{7,3},{8,12},{9,13},{10,... | collective-permute-start | bytes 98312 | tf_op jit(solution)/shard_map/ppermute | solution.py:1444
  71.0 8.2 %collective-permute-start.18 = (f32[64,128]{1,0:T(8,128)S(1)}, f32[64,128]{1,0:T(8,128)S(1)}, u32[]{:S(2)}, u32[]{:S(2)}) collective-permute-start(f32[64,128]{1,0:T(8,128)S(1)} %add.37.refs_4_), channel_id=1, source_target_pairs={{0,6},{1,7},{2,4},{3,5},{4,2},{5,3},{6,0},{7,1},{8,14},{9,15},{10,... | collective-permute-start | bytes 98312 | tf_op jit(solution)/shard_map/ppermute | solution.py:1444
  79.3 19.9 %all-to-all-start = ((bf16[8,9,36,128]{3,2,1,0:T(8,128)(2,1)}), bf16[8,9,36,128]{3,2,1,0:T(8,128)(2,1)S(1)}, u32[]{:S(2)}, u32[]{:S(2)}) async-start(bf16[8,9,36,128]{3,2,1,0:T(8,128)(2,1)} %get-tuple-element.99), calls=%async_computation | async-start | bytes 1474560 | tf_op jit(solution)/shard_map/all_to_all | solution.py:1439
  82.9 7.4 %collective-permute-start.19 = (bf16[11,32,128]{2,1,0:T(8,128)(2,1)S(1)}, bf16[11,32,128]{2,1,0:T(8,128)(2,1)S(1)}, u32[]{:S(2)}, u32[]{:S(2)}) collective-permute-start(bf16[11,32,128]{2,1,0:T(8,128)(2,1)S(1)} %get-tuple-element.101), channel_id=1, source_target_pairs={{0,8},{8,16},{16,24},{24,0},{1,9},{9,17},{17,25},{25,1},{2,10},{10... | collective-permute-start | bytes 270344 | tf_op jit(solution)/shard_map/ppermute | solution.py:1554
  84.6 9.1 %collective-permute-start.20 = (bf16[11,32,128]{2,1,0:T(8,128)(2,1)S(1)}, bf16[11,32,128]{2,1,0:T(8,128)(2,1)S(1)}, u32[]{:S(2)}, u32[]{:S(2)}) collective-permute-start(bf16[11,32,128]{2,1,0:T(8,128)(2,1)S(1)} %get-tuple-element.102), channel_id=1, source_target_pairs={{0,16},{8,24},{16,0},{24,8},{1,17},{9,25},{17,1},{25,9},{2,18},{10... | collective-permute-start | bytes 270344 | tf_op jit(solution)/shard_map/ppermute | solution.py:1554
  87.2 6.5 %collective-permute-start.21 = (bf16[11,32,128]{2,1,0:T(8,128)(2,1)S(1)}, bf16[11,32,128]{2,1,0:T(8,128)(2,1)S(1)}, u32[]{:S(2)}, u32[]{:S(2)}) collective-permute-start(bf16[11,32,128]{2,1,0:T(8,128)(2,1)S(1)} %get-tuple-element.103), channel_id=1, source_target_pairs={{0,24},{8,0},{16,8},{24,16},{1,25},{9,1},{17,9},{25,17},{2,26},{10... | collective-permute-start | bytes 270344 | tf_op jit(solution)/shard_map/ppermute | solution.py:1554
  94.5 16.3 %collective-permute-start.22 = (bf16[11,32,128]{2,1,0:T(8,128)(2,1)S(1)}, bf16[11,32,128]{2,1,0:T(8,128)(2,1)S(1)}, u32[]{:S(2)}, u32[]{:S(2)}) collective-permute-start(bf16[11,32,128]{2,1,0:T(8,128)(2,1)S(1)} %get-tuple-element.109.refs_0_), channel_id=1, source_target_pairs={{0,8},{8,16},{16,24},{24,0},{1,9},{9,17},{17,25},{25,1},{2,10},{10... | collective-permute-start | bytes 270344 | tf_op jit(solution)/shard_map/ppermute | solution.py:1564
  96.9 13.9 %collective-permute-start.23 = (bf16[11,32,128]{2,1,0:T(8,128)(2,1)S(1)}, bf16[11,32,128]{2,1,0:T(8,128)(2,1)S(1)}, u32[]{:S(2)}, u32[]{:S(2)}) collective-permute-start(bf16[11,32,128]{2,1,0:T(8,128)(2,1)S(1)} %get-tuple-element.109.refs_0_), channel_id=1, source_target_pairs={{0,16},{8,24},{16,0},{24,8},{1,17},{9,25},{17,1},{25,9},{2,18},{10... | collective-permute-start | bytes 270344 | tf_op jit(solution)/shard_map/ppermute | solution.py:1564
  98.5 12.3 %collective-permute-start.24 = (bf16[11,32,128]{2,1,0:T(8,128)(2,1)S(1)}, bf16[11,32,128]{2,1,0:T(8,128)(2,1)S(1)}, u32[]{:S(2)}, u32[]{:S(2)}) collective-permute-start(bf16[11,32,128]{2,1,0:T(8,128)(2,1)S(1)} %get-tuple-element.109.refs_0_), channel_id=1, source_target_pairs={{0,24},{8,0},{16,8},{24,16},{1,25},{9,1},{17,9},{25,17},{2,26},{10... | collective-permute-start | bytes 270344 | tf_op jit(solution)/shard_map/ppermute | solution.py:1564
  99.3 11.5 %all-to-all-start.1 = ((f32[32,1,128]{2,1,0:T(1,128)}), f32[32,1,128]{2,1,0:T(1,128)S(1)}, u32[]{:S(2)}, u32[]{:S(2)}) async-start(f32[32,1,128]{2,1,0:T(1,128)} %get-tuple-element.106), calls=%async_computation.1 | async-start | bytes 32768 | tf_op jit(solution)/shard_map/all_to_all | solution.py:1439
  104.9 11.1 %copy-start.4 = (f32[656]{0:T(1024)S(1)}, f32[656]{0:T(1024)}, u32[]{:S(2)}) copy-start(f32[656]{0:T(1024)} %param.21) | copy-start | bytes 7876
  115.9 0.7 copy-start.2
